TPU v7x, 32 devices: a whole 2x2x4 slice. The times are simulated.
32 devices in a mesh: cyl: 2 (over y), chain: 4 (over z), tensor: 4 (over x, core).
Axes of the slice: x: 2, y: 2, z: 4, core: 2. Of those that a mesh axis runs over, the one named last changes fastest.
Arguments:
- env: bfloat16 [8, 32, 10, 128, 128], P(('cyl', 'chain'), 'tensor'), parts along dimension 0, may hold values from -8 to 8, as said below
- site: bfloat16 [8, 32, 128, 128], P(('cyl', 'chain'), 'tensor'), parts along dimension 0, may hold values from -0.5 to 0.5
- seg_weight: float32 [8, 32, 128], P(('cyl', 'chain'), 'tensor'), parts along dimension 0, may hold values from 0.7 to 1.4
- ranks: int32 [64], P(('cyl', 'tensor')), parts along dimension 0, may hold values from 32 to 128
- mpo_mask: int32 [64, 10], P(('cyl', 'tensor')), parts along dimension 0, may hold values 0 or 1
Outputs:
- psi: bfloat16 [8, 32, 128, 128], P(('cyl', 'chain'), 'tensor'), parts along dimension 0
- energy: float32 [8], P(('cyl', 'chain')), parts along dimension 0
There are 2 independent parts, one for each index of `cyl`. A program takes and returns all parts, laid end to end along the dimension named above; each array names one. Nothing has to cross between parts.
Inputs may be any that keep to these rules, and one draw needn't show every extreme that they name: `env`: every environment block is symmetric in its last two dimensions.
All inputs are finite; a program needn't handle non-finite values. No bound on the sum of `mpo_mask` on one device may be relied on, other than what follows from the above.
Results may differ from a plain program's by a relative error of at most 0.011.
Values may be sent and summed in bfloat16 or wider, within the bound.
No kernel may reach another device: no remote copies, remote signals or barrier semaphores. Data moves between devices by JAX's collectives and lax.ppermute only.
A program may use at most 192 MiB of HBM per device.

v0:
```python
import functools

import jax
import jax.numpy as jnp
from jax import lax
from jax.experimental import pallas as pl
from jax.experimental.pallas import tpu as pltpu
from jax.sharding import PartitionSpec as P

ITERS = 4
STEP_SIZE = 0.5
PACK_COST = 10**7
REST_COST = 10**10
OWN_COST = 0
EPS = 1e-6
BF16 = jnp.bfloat16
F32 = jnp.float32
VMEM_LIMIT = 16 * 2**20
VM = pl.BlockSpec(memory_space=pltpu.VMEM)
SM = pl.BlockSpec(memory_space=pltpu.SMEM)


def params():
    return pltpu.CompilerParams(vmem_limit_bytes=VMEM_LIMIT)


def cost(flops, bytes_accessed):
    return pl.CostEstimate(flops=int(flops), bytes_accessed=int(bytes_accessed), transcendentals=0)


def vmem(shape, dtype):
    return pltpu.VMEM(shape, dtype)


def keep(x):
    return pltpu.with_memory_space_constraint(x, pltpu.VMEM)


def keep_scalars(x):
    return pltpu.with_memory_space_constraint(x, pltpu.SMEM)


def stay(x):
    return pltpu.with_memory_space_constraint(x, pltpu.HBM)


def grid_ij(edge):
    i = lax.broadcasted_iota(jnp.int32, (edge, edge), 0)
    j = lax.broadcasted_iota(jnp.int32, (edge, edge), 1)
    return i, j


def diag_row(block, i, j):
    return jnp.sum(jnp.where(i == j, block, 0.0), axis=0, keepdims=True)


SOURCE, SECTOR, PLACE, TARGET, RANK, COUNT, NUMBER, END = range(8)


def pack(cut, group, table, env, rows_ref, out, before=lambda g, carry: carry, after=None, carry=0):
    low, high = cut
    edge = env.shape[-1]
    i, j = grid_ij(edge)

    def body(g, carry):
        carry = before(g, carry)
        for d in range(group):
            p = g * group + d
            first = env[table[SOURCE, 2 * p]].astype(F32)
            second = env[table[SOURCE, 2 * p + 1]].astype(F32)
            at = pl.multiple_of((p - low) * edge, edge)
            out[pl.ds(at, edge), :] = jnp.where(i <= j, first, second).astype(BF16)
            rows_ref[pl.ds(2 * (p - low), 1), :] = diag_row(first, i, j)
            rows_ref[pl.ds(2 * (p - low) + 1, 1), :] = diag_row(second, i, j)
        if after is not None:
            after(g)
        return carry

    pairs = (table[NUMBER, 0] + 1) // 2
    stop = (jnp.minimum(high, pairs) + group - 1) // group
    carry = lax.fori_loop(low // group, stop, body, carry)
    size = (high - low) * edge
    out[size:, :] = rows_ref[: out.shape[0] - size, :].astype(BF16)
    return carry


def split_rows(value):
    high = value.astype(BF16).astype(F32)
    middle = (value - high).astype(BF16).astype(F32)
    low = value - high - middle
    pad = jnp.zeros((weight_rows(value.shape[0]) - 3 * value.shape[0], value.shape[1]), F32)
    return jnp.concatenate([high, middle, low, pad], axis=0).astype(BF16)


def joined_rows(rows, sectors):
    rows = rows.astype(F32)
    return rows[:sectors] + rows[sectors : 2 * sectors] + rows[2 * sectors : 3 * sectors]


def weight_rows(sectors):
    return -(-3 * sectors // 16) * 16


def pack_kernel(cut, overs, group, mask_hbm, ranks_hbm, weight_hbm, env_hbm, *refs):
    over_hbm, refs = refs[: len(overs)], refs[len(overs) :]
    out_hbm, table, flag, env, out, spare, mask_ref, ranks_ref, weight_ref, rows_ref = refs[:10]
    scalar_sems, sems, out_sems, over_sem = refs[10:]
    sectors, chans = mask_ref.shape
    blocks = sectors * chans
    scalars = [
        pltpu.make_async_copy(mask_hbm, mask_ref, scalar_sems.at[0]),
        pltpu.make_async_copy(ranks_hbm, ranks_ref, scalar_sems.at[1]),
        pltpu.make_async_copy(weight_hbm, weight_ref, scalar_sems.at[2]),
    ]
    for c in scalars:
        c.start()

    def fetch(s):
        part = pl.ds(s * chans, chans)
        return pltpu.make_async_copy(env_hbm.at[part], env.at[part], sems.at[s])

    for s in range(sectors):
        fetch(s).start()
    for c in scalars:
        c.wait()
    n = jnp.int32(0)
    for s in range(sectors):
        table[RANK, s] = ranks_ref[s]
        k = jnp.int32(0)
        for w in range(chans):
            m = mask_ref[s, w]
            table[SOURCE, n] = jnp.int32(s * chans + w)
            table[SECTOR, n] = jnp.int32(s)
            table[PLACE, n] = k
            table[TARGET, n] = s * chans + k
            n = n + m
            k = k + m
        table[COUNT, s] = k
    for d in range(2 * group):
        table[SOURCE, n + d] = jnp.int32(0)
        table[SECTOR, n + d] = jnp.int32(0)
        table[PLACE, n + d] = jnp.int32(chans)
        table[TARGET, n + d] = jnp.int32(blocks)
    table[NUMBER, 0] = n
    flag[0] = n

    def wait(s, carry):
        fetch(s).wait()
        return carry

    def before(g, here):
        final = jnp.maximum(jnp.minimum(2 * (g + 1) * group, n) - 1, 0)
        need = jnp.maximum(here, table[SECTOR, final] + 1)
        lax.fori_loop(here, need, wait, 0)
        return need

    extra = weight_rows(sectors)
    edge = env.shape[-1]
    size = (cut[1] - cut[0]) * edge
    out[out.shape[0] - extra :, :] = split_rows(weight_ref[...])
    bulk = out.at[: out.shape[0] - extra, :]

    def send(g):
        part = pl.ds(pl.multiple_of(g * group * edge, group * edge), group * edge)
        return pltpu.make_async_copy(out.at[part], out_hbm.at[part], out_sems.at[g])

    def after(g):
        send(g).start()

    here = pack(cut, group, table, env, rows_ref, bulk, before, after, jnp.int32(0))
    tail = pltpu.make_async_copy(out.at[size:], out_hbm.at[size:], out_sems.at[cut[1] // group])
    tail.start()
    lax.fori_loop(here, sectors, wait, 0)
    for over, to in zip(overs, over_hbm):

        @pl.when(n > 2 * over[0])
        def _(over=over, to=to):
            part = spare.at[: to.shape[0]]
            pack(over, group, table, env, rows_ref, part)
            copy = pltpu.make_async_copy(part, to, over_sem)
            copy.start()
            copy.wait()

    tail.wait()

    def drain(g, carry):
        send(g).wait()
        return carry

    stop = (jnp.minimum(cut[1], (n + 1) // 2) + group - 1) // group
    lax.fori_loop(0, stop, drain, 0)


def rest_kernel(cuts, group, table, env, *refs):
    chunks, rows_ref = refs[-len(cuts) - 1 : -1], refs[-1]
    for cut, out in zip(cuts, chunks):
        pack(cut, group, table, env, rows_ref, out)


def put(k, block, side, table, outer, buf):
    buf[side, table[TARGET, k]] = (block * outer[table[SECTOR, k]]).astype(BF16)


def put_diag(k, row, side, table, outer_diag, diags):
    s = table[SECTOR, k]
    scaled = row * outer_diag[pl.ds(s, 1), :]
    diags[side, s, pl.ds(table[PLACE, k], 1), :] = scaled.astype(BF16).astype(F32)


def unpack(cut, group, side, chunk, table, outer, outer_diag, buf, diags, rows_ref):
    low, high = cut
    edge = chunk.shape[-1]
    i, j = grid_ij(edge)
    n = table[NUMBER, 0]
    size = (high - low) * edge
    rows_ref[: chunk.shape[0] - size, :] = chunk[size:, :].astype(F32)

    def body(g, carry):
        for d in range(group):
            p = g * group + d
            at = pl.multiple_of((p - low) * edge, edge)
            both = chunk[pl.ds(at, edge), :].astype(F32)
            flip = both.T
            row = rows_ref[pl.ds(2 * (p - low), 1), :]
            other = rows_ref[pl.ds(2 * (p - low) + 1, 1), :]
            put(2 * p, jnp.where(i <= j, both, flip), side, table, outer, buf)
            lower = jnp.where(i > j, both, jnp.where(i == j, other, flip))
            put(2 * p + 1, lower, side, table, outer, buf)
            put_diag(2 * p, row, side, table, outer_diag, diags)
            put_diag(2 * p + 1, other, side, table, outer_diag, diags)
        return carry

    stop = (jnp.minimum(high, (n + 1) // 2) + group - 1) // group
    lax.fori_loop(low // group, stop, body, 0)


def widths(sectors, chans):
    parts = [10 if p < -(-sectors // 8) else 8 if p < sectors // 2 else 6 for p in range(sectors)]
    return [min(chans, -(-chans * part // 20) * 2) for part in parts]


def make_plan(plan, table, caps, chans):
    sectors = len(caps)
    counts = [table[COUNT, s] for s in range(sectors)]
    places = []
    for s in range(sectors):
        place = jnp.int32(0)
        for t in range(sectors):
            if t != s:
                ahead = counts[t] >= counts[s] if t < s else counts[t] > counts[s]
                place = place + ahead.astype(jnp.int32)
        plan[COUNT, place] = jnp.int32(s)
        plan[RANK, place] = table[RANK, s]
        places.append(place)
    fits = jnp.int32(1)
    for k, cap in enumerate(caps):
        fits = fits * (table[COUNT, plan[COUNT, k]] <= cap).astype(jnp.int32)
    n = table[NUMBER, 0]
    plan[NUMBER, 0] = n
    plan[NUMBER, 1] = fits
    start = jnp.int32(0)
    for s in range(sectors):

        def body(c, k, s=s):
            plan[SOURCE, k] = table[SOURCE, k]
            plan[SECTOR, k] = places[s]
            plan[PLACE, k] = c
            plan[TARGET, k] = places[s] * chans + c
            return k + 1

        start = lax.fori_loop(0, counts[s], body, start)
        plan[END, places[s]] = start

    def rest(k, carry):
        for row in (SOURCE, SECTOR, PLACE, TARGET):
            plan[row, k] = table[row, k]
        return carry

    lax.fori_loop(n, n + table.shape[1] - sectors * chans, rest, 0)


def own_kernel(group, chans, table, env, own_site, other_site, *refs):
    weights, (buf, diags, prefix, vec, plan, mine, rows_ref) = refs[:-7], refs[-7:]
    sectors, edge = mine.shape[0], mine.shape[-1]
    make_plan(plan, table, widths(sectors, chans), chans)
    at = lax.axis_index("chain")
    side = at % 2
    before = jnp.ones((sectors, edge), F32)
    for c in range(len(weights) + 1):
        value = before
        for d, weight in enumerate(weights[1:], 2):
            value = jnp.where(at ^ d == c, weight[...], value)
        before = jnp.where(c < at - side, before * value, before)
    prefix[...] = before
    own_weight = weights[0][...]
    rows_ref[...] = jnp.where(side == 0, before * own_weight, own_weight)
    i, j = grid_ij(edge)
    for s in range(sectors):
        old = plan[COUNT, s]
        row = jnp.broadcast_to(rows_ref[pl.ds(old, 1), :], (edge, edge))
        mine[s] = row.T * row
        first = jnp.where(side == 0, own_site[old], other_site[old])
        second = jnp.where(side == 0, other_site[old], own_site[old])
        start = jnp.dot(first, second, preferred_element_type=F32).T
        vec[s] = jnp.where(j < plan[RANK, s], start, 0.0)
    diags[...] = jnp.zeros_like(diags)

    def wipe(t, carry):
        buf[0, t] = jnp.zeros((edge, edge), BF16)
        buf[1, t] = jnp.zeros((edge, edge), BF16)
        return carry

    lax.fori_loop(0, sectors * chans, wipe, 0)
    step = 2 * group

    def body(g, carry):
        for d in range(step):
            k = step * g + d
            s = plan[SECTOR, k]
            block = (env[plan[SOURCE, k]].astype(F32) * mine[s]).astype(BF16)
            buf[side, plan[TARGET, k]] = block
            diags[side, s, pl.ds(plan[PLACE, k], 1), :] = diag_row(block.astype(F32), i, j)
        return carry

    lax.fori_loop(0, (plan[NUMBER, 0] + step - 1) // step, body, 0)


def outer_kernel(cut, group, plan, prefix, chunk, *refs):
    _, _, buf, diags, outer, outer_diag, rows_ref, weight_ref = refs
    sectors, edge = outer.shape[0], outer.shape[-1]
    side = lax.axis_index("chain") % 2
    extra = weight_rows(sectors)
    start = chunk.shape[0] - extra
    other_weight = joined_rows(chunk[start:, :], sectors)
    weight_ref[...] = jnp.where(side == 0, other_weight, prefix[...] * other_weight)
    for s in range(sectors):
        row = weight_ref[pl.ds(plan[COUNT, s], 1), :]
        outer_diag[s : s + 1, :] = row * row
        row = jnp.broadcast_to(row, (edge, edge))
        outer[s] = row.T * row
    bulk = chunk.at[:start, :]
    unpack(cut, group, 1 - side, bulk, plan, outer, outer_diag, buf, diags, rows_ref)


def mid_kernel(cut, group, plan, outer, outer_diag, vec, chunk, *refs):
    _, _, buf, diags, image, inner, rows_ref = refs
    side = lax.axis_index("chain") % 2
    unpack(cut, group, 1 - side, chunk, plan, outer, outer_diag, buf, diags, rows_ref)
    sectors, chans = vec.shape[0], inner.shape[-1] // vec.shape[-1]
    for few, caps in ((1, widths(sectors, chans)), (0, [chans] * sectors)):

        @pl.when(plan[NUMBER, 1] == few)
        def _(caps=caps):
            all_images(caps, plan, buf, vec, image, inner)


def all_images(caps, plan, buf, vec, image, inner):
    edge = vec.shape[-1]
    chans = inner.shape[-1] // edge
    _, j = grid_ij(edge)
    for s, cap in enumerate(caps):
        right = buf[1, s * chans : s * chans + cap].reshape(cap * edge, edge)
        image_t = jnp.dot(right, vec[s].astype(BF16), preferred_element_type=F32).astype(BF16)
        for c in range(cap):
            inner[s, :, c * edge : (c + 1) * edge] = image_t[c * edge : (c + 1) * edge]
    for s, cap in enumerate(caps):
        left = buf[0, s * chans : s * chans + cap].reshape(cap * edge, edge)
        hv = jnp.dot(inner[s, :, : cap * edge], left, preferred_element_type=F32)
        image[s] = jnp.where(j < plan[RANK, s], hv, 0.0)


def late_images(low, plan, buf, vec, image, inner):
    sectors, edge = vec.shape[0], vec.shape[-1]
    chans = inner.shape[-1] // edge
    _, j = grid_ij(edge)
    fits = plan[NUMBER, 1]
    for s, cap in enumerate(widths(sectors, chans)):
        take = plan[END, s] > low
        for few, width in ((1, cap), (0, chans)):

            @pl.when(jnp.logical_and(take, fits == few))
            def _(s=s, width=width):
                one_image(s, width, plan, buf, vec[s], image, inner, j)


def one_image(s, width, plan, buf, vector, image, inner, j):
    edge = vector.shape[-1]
    chans = inner.shape[-1] // edge
    right = buf[1, s * chans : s * chans + width].reshape(width * edge, edge)
    image_t = jnp.dot(right, vector.astype(BF16), preferred_element_type=F32).astype(BF16)
    for c in range(width):
        inner[s, :, c * edge : (c + 1) * edge] = image_t[c * edge : (c + 1) * edge]
    left = buf[0, s * chans : s * chans + width].reshape(width * edge, edge)
    hv = jnp.dot(inner[s, :, : width * edge], left, preferred_element_type=F32)
    image[s] = jnp.where(j < plan[RANK, s], hv, 0.0)


def apply_all(vectors, plan, *state):
    vec, inner = state[1], state[-1]
    sectors, chans = vec.shape[0], inner.shape[-1] // vec.shape[-1]
    fits = plan[NUMBER, 1]

    @pl.when(fits == 1)
    def _():
        apply_some(vectors, plan, widths(sectors, chans), *state)

    @pl.when(fits == 0)
    def _():
        apply_some(vectors, plan, [chans] * sectors, *state)


def apply_some(vectors, plan, caps, buf, vec, image, part, inner):
    sectors, edge = vec.shape[0], vec.shape[-1]
    chans = inner.shape[-1] // edge
    for s, cap in enumerate(caps):
        vector = vectors(s)
        vec[s] = vector
        right = buf[1, s * chans : s * chans + cap].reshape(cap * edge, edge)
        image_t = jnp.dot(right, vector.astype(BF16), preferred_element_type=F32).astype(BF16)
        for c in range(cap):
            inner[s, :, c * edge : (c + 1) * edge] = image_t[c * edge : (c + 1) * edge]
    _, j = grid_ij(edge)
    along = jnp.zeros((edge, edge), F32)
    square = jnp.zeros((edge, edge), F32)
    for s, cap in enumerate(caps):
        left = buf[0, s * chans : s * chans + cap].reshape(cap * edge, edge)
        hv = jnp.dot(inner[s, :, : cap * edge], left, preferred_element_type=F32)
        hv = jnp.where(j < plan[RANK, s], hv, 0.0)
        image[s] = hv
        vector = vec[s]
        along = along + vector * hv
        square = square + vector * vector
    store_sums(part, along, square)


def store_sums(part, along, square):
    part[0:1, :] = jnp.sum(along, axis=0, keepdims=True)
    part[1:2, :] = jnp.sum(square, axis=0, keepdims=True)


def first_kernel(cuts, group, plan, outer, outer_diag, vec, chunk, *refs):
    overs, refs = refs[: len(cuts) - 1], refs[len(cuts) - 1 :]
    _, _, _, buf, diags, image, part, inner, rows_ref, spare, sem = refs
    sectors = vec.shape[0]
    side = lax.axis_index("chain") % 2
    unpack(cuts[0], group, 1 - side, chunk, plan, outer, outer_diag, buf, diags, rows_ref)
    for cut, over in zip(cuts[1:], overs):

        @pl.when(plan[NUMBER, 0] > 2 * cut[0])
        def _(cut=cut, over=over):
            here = spare.at[: over.shape[0]]
            copy = pltpu.make_async_copy(over, here, sem)
            copy.start()
            copy.wait()
            unpack(cut, group, 1 - side, here, plan, outer, outer_diag, buf, diags, rows_ref)

    late_images(2 * cuts[0][0], plan, buf, vec, image, inner)
    along = jnp.zeros(vec.shape[1:], F32)
    square = along
    for s in range(sectors):
        along = along + vec[s] * image[s]
        square = square + vec[s] * vec[s]
    store_sums(part, along, square)


def diag_kernel(chans, diags, dh):
    used = lax.broadcasted_iota(jnp.int32, diags.shape[2:], 0) < chans
    for s in range(dh.shape[0]):
        dh[s] = lax.dot_general(
            jnp.where(used, diags[1, s], 0.0).astype(BF16),
            jnp.where(used, diags[0, s], 0.0).astype(BF16),
            (((0,), (0,)), ((), ())),
            preferred_element_type=F32,
        )


def joined(parts):
    values = [p[...] for p in parts]
    while len(values) > 1:
        values = [values[k] + values[k + 1] for k in range(0, len(values), 2)]
    total = values[0]
    along = jnp.sum(total[0:1, :], axis=1, keepdims=True)
    square = jnp.sum(total[1:2, :], axis=1, keepdims=True)
    return along, square


def step_of(count, along, square):
    theta = along / (square + EPS)
    scale = 1.0 / jnp.sqrt(square / count + EPS)

    def step(vector, hv, dh):
        resid = hv - theta * vector
        return (vector - STEP_SIZE * resid / (1.0 + jnp.abs(dh - theta))) * scale

    return theta, step


def iter_kernel(count, partners, plan, buf, vec_in, image_in, dh, *refs):
    parts = refs[:partners]
    vec, image, part, inner = refs[partners:]
    _, step = step_of(count, *joined(parts))
    apply_all(
        lambda s: step(vec_in[s], image_in[s], dh[s]), plan, buf, vec, image, part, inner
    )


def last_kernel(count, partners, vec_in, image_in, dh, *refs):
    parts = refs[:partners]
    vec, part, energy = refs[partners:]
    theta, step = step_of(count, *joined(parts))
    square = jnp.zeros(dh.shape[1:], F32)
    for s in range(dh.shape[0]):
        vector = step(vec_in[s], image_in[s], dh[s])
        vec[s] = vector
        square = square + vector * vector
    store_sums(part, square, square)
    energy[...] = jnp.broadcast_to(theta, energy.shape)


def turn_kernel(vec, turned):
    for s in range(vec.shape[0]):
        turned[s] = vec[s].T


def psi_kernel(count, partners, plan, vec, *refs):
    parts = refs[:partners]
    psi, ready, sems = refs[partners:]
    square, _ = joined(parts)
    scale = 1.0 / jnp.sqrt(square / count + EPS)
    copies = []
    for s in range(psi.shape[0]):
        ready[s] = (vec[s] * scale).astype(BF16)
        copies.append(pltpu.make_async_copy(ready.at[s], psi.at[plan[COUNT, s]], sems.at[s]))
        copies[-1].start()
    for copy in copies:
        copy.wait()


def swap(value):
    return swapped(value, "chain", 1)


def swapped(value, axis, mask):
    size = lax.axis_size(axis)
    return lax.ppermute(value, axis, [(k, k ^ mask) for k in range(size)])


def from_all(value, axis):
    return [value] + [swapped(value, axis, m) for m in range(1, lax.axis_size(axis))]


def gather_parts(part):
    return [keep(p) for p in from_all(part, "tensor")]


def local(env, site, seg_weight, ranks, mpo_mask):
    sectors, chans, edge = env.shape[1:4]
    blocks = sectors * chans
    tensor = lax.axis_size("tensor")
    count = float(sectors * tensor * edge * edge)
    group = 4
    pairs = -(-blocks // (2 * group)) * group
    base = min(pairs, -(-pairs * 3 // 5 // (2 * group)) * 2 * group)
    third = max(base // 6 // group, 1) * group
    marks = [0, base // 2, base - third, base, min(base + third, pairs), pairs]
    cuts = [(a, b) for a, b in zip(marks[:-1], marks[1:]) if a < b]
    usual = 3
    tails = [-(-2 * (c[1] - c[0]) // 16) * 16 for c in cuts]
    rows = [(c[1] - c[0]) * edge + t for c, t in zip(cuts, tails)]
    rows[0] += weight_rows(sectors)
    block_bytes = 2 * edge * edge
    big = sectors * edge * edge * 4

    own_weight = seg_weight[0]
    weights = [swapped(own_weight, "chain", m) for m in range(2, lax.axis_size("chain"))]
    other_site = swap(site[0])
    flat_env = env.reshape(blocks, edge, edge)
    state_shape = (sectors, edge, edge)
    state = vmem(state_shape, F32)
    row_shape = vmem((sectors, edge), F32)
    table_shape = pltpu.SMEM((8, blocks + 2 * group), jnp.int32)

    hbm = pl.BlockSpec(memory_space=pltpu.HBM)
    dma = pltpu.SemaphoreType.DMA
    tail_rows = pltpu.VMEM((max(tails), edge), F32)
    *overs, first_sent, table, active, env_here = pl.pallas_call(
        functools.partial(pack_kernel, cuts[0], cuts[usual:], group),
        out_shape=[jax.ShapeDtypeStruct((r, edge), BF16) for r in rows[usual:]]
        + [
            jax.ShapeDtypeStruct((rows[0], edge), BF16),
            table_shape,
            pltpu.SMEM((1,), jnp.int32),
            vmem((blocks, edge, edge), BF16),
        ],
        in_specs=[hbm] * 4,
        out_specs=[hbm] * len(cuts[usual:]) + [hbm, SM, SM, VM],
        scratch_shapes=[
            pltpu.VMEM((rows[0], edge), BF16),
            pltpu.VMEM((max(rows[usual:]), edge), BF16),
            pltpu.SMEM(mpo_mask.shape, jnp.int32),
            pltpu.SMEM(ranks.shape, jnp.int32),
            pltpu.VMEM((sectors, edge), F32),
            tail_rows,
            dma((3,)),
            dma((sectors,)),
            dma((cuts[0][1] // group + 1,)),
            dma(()),
        ],
        compiler_params=params(),
        cost_estimate=cost(PACK_COST, 2 * blocks * block_bytes),
        name="pack",
    )(stay(mpo_mask), stay(ranks), stay(own_weight), stay(flat_env))
    table, env_here = keep_scalars(table), keep(env_here)

    def send(k):
        if k == len(overs):
            return []
        moved = functools.partial(lambda x: [swap(x)], overs[k])
        return lax.cond(
            active[0] > 2 * cuts[usual + k][0],
            lambda: moved() + send(k + 1),
            lambda: list(overs[k:]),
        )

    extra = [stay(x) for x in send(0)]
    sent = pl.pallas_call(
        functools.partial(rest_kernel, cuts[1:usual], group),
        out_shape=[vmem((r, edge), BF16) for r in rows[1:usual]],
        in_specs=[SM, VM] + [hbm] * (1 + len(extra) + len(weights)),
        out_specs=[VM] * (usual - 1),
        scratch_shapes=[tail_rows],
        compiler_params=params(),
        cost_estimate=cost(REST_COST, 2 * blocks * block_bytes),
        name="rest",
    )(table, env_here, *extra, stay(other_site), *[stay(w) for w in weights])
    got = [keep(swap(c)) for c in (first_sent, *sent)]

    buf_shape = vmem((2, blocks + 1, edge, edge), BF16)
    diag_shape = vmem((2, sectors, -(-(chans + 1) // 16) * 16, edge), F32)
    sums = vmem((2, edge), F32)
    inner_shape = pltpu.VMEM((sectors, edge, chans * edge), BF16)
    work = 4.0 * blocks * edge**3

    buf, diags, prefix, vec, plan = pl.pallas_call(
        functools.partial(own_kernel, group, chans),
        out_shape=[buf_shape, diag_shape, row_shape, state, table_shape],
        in_specs=[SM] + [VM] * (4 + len(weights)),
        out_specs=[VM] * 4 + [SM],
        scratch_shapes=[pltpu.VMEM(state_shape, F32), pltpu.VMEM((sectors, edge), F32)],
        compiler_params=params(),
        cost_estimate=cost(OWN_COST, 0),
        name="own",
    )(table, env_here, site[0], stay(other_site), own_weight, *[stay(w) for w in weights])
    plan = keep_scalars(plan)

    buf, diags, outer, outer_diag = pl.pallas_call(
        functools.partial(outer_kernel, cuts[0], group),
        out_shape=[buf_shape, diag_shape, state, row_shape],
        in_specs=[SM] + [VM] * 4,
        out_specs=[VM] * 4,
        scratch_shapes=[tail_rows, pltpu.VMEM((sectors, edge), F32)],
        input_output_aliases={3: 0, 4: 1},
        compiler_params=params(),
        cost_estimate=cost(0, 0),
        name="outer",
    )(plan, keep(prefix), got[0], keep(buf), keep(diags))

    buf, diags, image = pl.pallas_call(
        functools.partial(mid_kernel, cuts[1], group),
        out_shape=[buf_shape, diag_shape, state],
        in_specs=[SM] + [VM] * 6,
        out_specs=[VM] * 3,
        scratch_shapes=[inner_shape, tail_rows],
        input_output_aliases={5: 0, 6: 1},
        compiler_params=params(),
        cost_estimate=cost(0, 0),
        name="mid",
    )(plan, keep(outer), keep(outer_diag), keep(vec), got[1], keep(buf), keep(diags))

    kept = 5 + len(extra)
    buf, diags, image, part = pl.pallas_call(
        functools.partial(first_kernel, cuts[usual - 1 :], group),
        out_shape=[buf_shape, diag_shape, state, sums],
        in_specs=[SM] + [VM] * 4 + [hbm] * len(extra) + [VM] * 3,
        out_specs=[VM] * 4,
        scratch_shapes=[
            inner_shape, tail_rows, pltpu.VMEM((max(rows[usual:]), edge), BF16), dma(()),
        ],
        input_output_aliases={kept: 0, kept + 1: 1, kept + 2: 2},
        compiler_params=params(),
        cost_estimate=cost(work, 2 * blocks * block_bytes),
        name="first",
    )(
        plan, keep(outer), keep(outer_diag), keep(vec), got[usual - 1], *extra,
        keep(buf), keep(diags), keep(image),
    )
    dh = pl.pallas_call(
        functools.partial(diag_kernel, chans),
        out_shape=state,
        in_specs=[VM],
        out_specs=VM,
        compiler_params=params(),
        cost_estimate=cost(0, 2 * big),
        name="diagonal",
    )(keep(diags))

    for _ in range(ITERS - 1):
        parts = gather_parts(part)
        vec, image, part = pl.pallas_call(
            functools.partial(iter_kernel, count, tensor),
            out_shape=[state, state, sums],
            in_specs=[SM] + [VM] * (4 + tensor),
            out_specs=[VM] * 3,
            scratch_shapes=[inner_shape],
            compiler_params=params(),
            cost_estimate=cost(work, 2 * blocks * block_bytes),
            name="iterate",
        )(plan, keep(buf), keep(vec), keep(image), keep(dh), *parts)

    parts = gather_parts(part)
    vec, part, energy = pl.pallas_call(
        functools.partial(last_kernel, count, tensor),
        out_shape=[state, sums, vmem((1, edge), F32)],
        in_specs=[VM] * (3 + tensor),
        out_specs=[VM] * 3,
        compiler_params=params(),
        cost_estimate=cost(0, 3 * big),
        name="last",
    )(keep(vec), keep(image), keep(dh), *parts)
    parts = gather_parts(part)
    turned = pl.pallas_call(
        turn_kernel,
        out_shape=state,
        in_specs=[VM],
        out_specs=VM,
        compiler_params=params(),
        cost_estimate=cost(0, 2 * big),
        name="turn",
    )(keep(vec))
    psi = pl.pallas_call(
        functools.partial(psi_kernel, count, tensor),
        out_shape=jax.ShapeDtypeStruct(state_shape, BF16),
        in_specs=[SM] + [VM] * (1 + tensor),
        out_specs=hbm,
        scratch_shapes=[pltpu.VMEM(state_shape, BF16), dma((sectors,))],
        compiler_params=params(),
        cost_estimate=cost(0, big),
        name="psi",
    )(plan, keep(turned), *parts)
    return psi[None], energy[0, :1]


def solution(mesh):
    in_specs = (
        P(("cyl", "chain"), "tensor", None, None, None),
        P(("cyl", "chain"), "tensor", None, None),
        P(("cyl", "chain"), "tensor", None),
        P(("cyl", "tensor")),
        P(("cyl", "tensor"), None),
    )
    out_specs = (P(("cyl", "chain"), "tensor", None, None), P(("cyl", "chain")))
    return jax.shard_map(local, mesh=mesh, in_specs=in_specs, out_specs=out_specs, check_vma=False)
```

profile of v0, /device:TPU:0, one launch (start us, length us, event | category | flops | bytes accessed | tf_op | source)
XLA Modules:
  0.0 54.2 jit_solution(16054744757975136361)
XLA Ops:
  0.6 3.1 %collective-permute-start.2 = (bf16[8,128,128]{2,1,0:T(8,128)(2,1)}, bf16[8,128,128]{2,1,0:T(8,128)(2,1)}, u32[]{:S(2)}, u32[]{:S(2)}) collective-permute-start(bf16[8,128,128]{2,1,0:T(8,128)(2,1)} %bitcast.8), channel_id=1, source_target_pairs={{0,4},{4,0},{8,12},{12,8},{1,5},{5,1},{9,13},{13,9},{2,6},{6,2},{1... | collective-permute-start | bytes 786440 | tf_op jit(solution)/shard_map/ppermute | solution.py:545
  3.7 2.5 %collective-permute-start.4 = (f32[8,128]{1,0:T(8,128)}, f32[8,128]{1,0:T(8,128)S(1)}, u32[]{:S(2)}, u32[]{:S(2)}) collective-permute-start(f32[8,128]{1,0:T(8,128)} %bitcast.10), channel_id=1, source_target_pairs={{0,12},{4,8},{8,4},{12,0},{1,13},{5,9},{9,5},{13,1},{2,14},{6,10},... | collective-permute-start | bytes 12296 | tf_op jit(solution)/shard_map/ppermute | solution.py:545
  6.2 0.1 collective-permute-start.3
  6.3 2.4 %pack.1 = (bf16[528,128]{1,0:T(8,128)(2,1)}, bf16[1568,128]{1,0:T(8,128)(2,1)S(1)}, bf16[1600,128]{1,0:T(8,128)(2,1)S(1)}, s32[8,88]{1,0:T(8,128)S(4)}, s32[1]{0:T(128)S(4)}, /*index=5*/bf16[80,128,128]{2,1,0:T(8,128)(2,1)S(1)}) custom-call(s32[8,10]{1,0:T(8,128)} %mask_hbm.1, s32[8]{0:T(128)} %ranks_hbm.1, f32[8,128]{1,0:T(8,128)} %bitcast.12, ...), custom_call_target="tpu_custom_call" | custom-call | flops 10000000 | bytes 5242880 | tf_op jit(solution)/shard_map/pack/pallas_call | solution.py:586
  8.8 0.0 copy-start.3
  8.8 1.9 %collective-permute-start.5 = (bf16[1600,128]{1,0:T(8,128)(2,1)S(1)}, bf16[1600,128]{1,0:T(8,128)(2,1)S(1)}, u32[]{:S(2)}, u32[]{:S(2)}) collective-permute-start(bf16[1600,128]{1,0:T(8,128)(2,1)S(1)} %get-tuple-element.62), channel_id=1, source_target_pairs={{0,4},{4,0},{8,12},{12,8},{1,5},{5,1},{9,13},{13,9},{2,6},{6,2},{1... | collective-permute-start | bytes 1228808 | tf_op jit(solution)/shard_map/ppermute | solution.py:545
  10.6 2.0 %collective-permute-done.4.refs_2_.refs_4_ = f32[8,128]{1,0:T(8,128)S(1)} collective-permute-done((f32[8,128]{1,0:T(8,128)}, f32[8,128]{1,0:T(8,128)S(1)}, u32[]{:S(2)}, u32[]{:S(2)}) %collective-permute-start.4) | collective-permute-done | bytes 4128 | tf_op jit(solution)/shard_map/ppermute | solution.py:545
  12.7 0.0 copy-start.4
  12.7 0.0 collective-permute-done.3.refs_1_.refs_3_
  12.7 0.0 collective-permute-done.2.other_site.refs_2_
  12.7 0.0 copy-done.3
  12.7 0.6 %copy-done.4 = f32[8,128]{1,0:T(8,128)} copy-done((f32[8,128]{1,0:T(8,128)}, f32[8,128]{1,0:T(8,128)S(1)}, u32[]{:S(2)}) %copy-start.4) | copy-done | bytes 4120
  13.3 0.0 copy-done.5
  13.3 0.3 rest.1
  13.6 0.5 %collective-permute-start.7 = (bf16[1040,128]{1,0:T(8,128)(2,1)S(1)}, bf16[1040,128]{1,0:T(8,128)(2,1)S(1)}, u32[]{:S(2)}, u32[]{:S(2)}) collective-permute-start(bf16[1040,128]{1,0:T(8,128)(2,1)S(1)} %get-tuple-element.74), channel_id=1, source_target_pairs={{0,4},{4,0},{8,12},{12,8},{1,5},{5,1},{9,13},{13,9},{2,6},{6,2},{1... | collective-permute-start | bytes 798728 | tf_op jit(solution)/shard_map/ppermute | solution.py:545
  14.1 1.5 %collective-permute-start.6 = (bf16[528,128]{1,0:T(8,128)(2,1)S(1)}, bf16[528,128]{1,0:T(8,128)(2,1)S(1)}, u32[]{:S(2)}, u32[]{:S(2)}) collective-permute-start(bf16[528,128]{1,0:T(8,128)(2,1)S(1)} %get-tuple-element.73), channel_id=1, source_target_pairs={{0,4},{4,0},{8,12},{12,8},{1,5},{5,1},{9,13},{13,9},{2,6},{6,2},{1... | collective-permute-start | bytes 405512 | tf_op jit(solution)/shard_map/ppermute | solution.py:545
  15.7 0.0 copy-done
  15.7 0.0 copy-done.1
  15.7 3.2 %own.1 = (bf16[2,81,128,128]{3,2,1,0:T(8,128)(2,1)S(1)}, f32[2,8,16,128]{3,2,1,0:T(8,128)S(1)}, f32[8,128]{1,0:T(8,128)S(1)}, f32[8,128,128]{2,1,0:T(8,128)S(1)}, s32[8,88]{1,0:T(8,128)S(4)}) custom-call(s32[8,88]{1,0:T(8,128)S(4)} %get-tuple-element.58.table, bf16[80,128,128]{2,1,0:T(8,128)(2,1)S(1)} %get-tuple-element.59.env, ...), custom_call_target="tpu_custom_call" | custom-call | tf_op jit(solution)/shard_map/own/pallas_call | solution.py:644
  18.9 2.4 %collective-permute-done.5.chunk = bf16[1600,128]{1,0:T(8,128)(2,1)S(1)} collective-permute-done((bf16[1600,128]{1,0:T(8,128)(2,1)S(1)}, bf16[1600,128]{1,0:T(8,128)(2,1)S(1)}, u32[]{:S(2)}, u32[]{:S(2)}) %collective-permute-start.5) | collective-permute-done | bytes 409632 | tf_op jit(solution)/shard_map/ppermute | solution.py:545
  21.3 0.7 %outer.1 = (bf16[2,81,128,128]{3,2,1,0:T(8,128)(2,1)S(1)}, f32[2,8,16,128]{3,2,1,0:T(8,128)S(1)}, f32[8,128,128]{2,1,0:T(8,128)S(1)}, f32[8,128]{1,0:T(8,128)S(1)}) custom-call(s32[8,88]{1,0:T(8,128)S(4)} %get-tuple-element.60.plan, f32[8,128]{1,0:T(8,128)S(1)} %get-tuple-element.61.prefix, ...), custom_call_target="tpu_custom_call", output_to_operand_aliasing={{0}: (3, {}), {1}: (4, {})} | custom-call | tf_op jit(solution)/shard_map/outer/pallas_call | solution.py:656
  22.0 4.8 %collective-permute-done.7.chunk = bf16[1040,128]{1,0:T(8,128)(2,1)S(1)} collective-permute-done((bf16[1040,128]{1,0:T(8,128)(2,1)S(1)}, bf16[1040,128]{1,0:T(8,128)(2,1)S(1)}, u32[]{:S(2)}, u32[]{:S(2)}) %collective-permute-start.7) | collective-permute-done | bytes 266272 | tf_op jit(solution)/shard_map/ppermute | solution.py:545
  26.8 1.5 %mid.1 = (bf16[2,81,128,128]{3,2,1,0:T(8,128)(2,1)S(1)}, f32[2,8,16,128]{3,2,1,0:T(8,128)S(1)}, f32[8,128,128]{2,1,0:T(8,128)S(1)}) custom-call(s32[8,88]{1,0:T(8,128)S(4)} %get-tuple-element.60.plan, f32[8,128,128]{2,1,0:T(8,128)S(1)} %get-tuple-element.65.outer, ...), custom_call_target="tpu_custom_call", output_to_operand_aliasing={{0}: (5, {}), {1}: (6, {})} | custom-call | tf_op jit(solution)/shard_map/mid/pallas_call | solution.py:668
  28.3 0.0 collective-permute-done.6.chunk
  28.3 1.1 %first.1 = (bf16[2,81,128,128]{3,2,1,0:T(8,128)(2,1)S(1)}, f32[2,8,16,128]{3,2,1,0:T(8,128)S(1)}, f32[8,128,128]{2,1,0:T(8,128)S(1)}, f32[2,128]{1,0:T(2,128)S(1)}) custom-call(s32[8,88]{1,0:T(8,128)S(4)} %get-tuple-element.60.plan, f32[8,128,128]{2,1,0:T(8,128)S(1)} %get-tuple-element.65.outer, ...), custom_call_target="tpu_custom_call", output_to_operand_aliasing={{0}: (7, {}), {1}: (8, {}), {2}: (9, {})} | custom-call | flops 671088640 | bytes 5242880 | tf_op jit(solution)/shard_map/first/pallas_call | solution.py:681
  29.4 0.1 collective-permute-start.10
  29.4 0.8 %collective-permute-start.9 = (f32[2,128]{1,0:T(2,128)S(1)}, f32[2,128]{1,0:T(2,128)S(1)}, u32[]{:S(2)}, u32[]{:S(2)}) collective-permute-start(f32[2,128]{1,0:T(2,128)S(1)} %get-tuple-element.83.refs_0_), channel_id=1, source_target_pairs={{0,2},{1,3},{2,0},{3,1},{4,6},{5,7},{6,4},{7,5},{8,10},{9,11},{10,... | collective-permute-start | bytes 3080 | tf_op jit(solution)/shard_map/ppermute | solution.py:545
  30.2 1.1 %collective-permute-start.8 = (f32[2,128]{1,0:T(2,128)S(1)}, f32[2,128]{1,0:T(2,128)S(1)}, u32[]{:S(2)}, u32[]{:S(2)}) collective-permute-start(f32[2,128]{1,0:T(2,128)S(1)} %get-tuple-element.83.refs_0_), channel_id=1, source_target_pairs={{0,1},{1,0},{2,3},{3,2},{4,5},{5,4},{6,7},{7,6},{8,9},{9,8},{10,11... | collective-permute-start | bytes 3080 | tf_op jit(solution)/shard_map/ppermute | solution.py:545
  31.3 0.3 diagonal.1.dh
  31.5 0.9 %collective-permute-done.10.refs_3_ = f32[2,128]{1,0:T(2,128)S(1)} collective-permute-done((f32[2,128]{1,0:T(2,128)S(1)}, f32[2,128]{1,0:T(2,128)S(1)}, u32[]{:S(2)}, u32[]{:S(2)}) %collective-permute-start.10) | collective-permute-done | bytes 1056 | tf_op jit(solution)/shard_map/ppermute | solution.py:545
  32.4 0.7 %collective-permute-done.9.refs_2_ = f32[2,128]{1,0:T(2,128)S(1)} collective-permute-done((f32[2,128]{1,0:T(2,128)S(1)}, f32[2,128]{1,0:T(2,128)S(1)}, u32[]{:S(2)}, u32[]{:S(2)}) %collective-permute-start.9) | collective-permute-done | bytes 1056 | tf_op jit(solution)/shard_map/ppermute | solution.py:545
  33.1 0.0 collective-permute-done.8.refs_1_
  33.1 1.3 %iterate.3 = (f32[8,128,128]{2,1,0:T(8,128)S(1)}, f32[8,128,128]{2,1,0:T(8,128)S(1)}, f32[2,128]{1,0:T(2,128)S(1)}) custom-call(s32[8,88]{1,0:T(8,128)S(4)} %get-tuple-element.60.plan, bf16[2,81,128,128]{3,2,1,0:T(8,128)(2,1)S(1)} %get-tuple-element.80.buf, f32[8,128,128]{2,1,0:T(8,128)S(1)} %get-tuple-element.67.vec.vec_in, ...), custom_call_target="tpu_custom_call" | custom-call | flops 671088640 | bytes 5242880 | tf_op jit(solution)/shard_map/iterate/pallas_call | solution.py:709
  34.4 0.6 %collective-permute-start.13 = (f32[2,128]{1,0:T(2,128)S(1)}, f32[2,128]{1,0:T(2,128)S(1)}, u32[]{:S(2)}, u32[]{:S(2)}) collective-permute-start(f32[2,128]{1,0:T(2,128)S(1)} %get-tuple-element.86.refs_0_), channel_id=1, source_target_pairs={{0,3},{1,2},{2,1},{3,0},{4,7},{5,6},{6,5},{7,4},{8,11},{9,10},{10,... | collective-permute-start | bytes 3080 | tf_op jit(solution)/shard_map/ppermute | solution.py:545
  35.0 0.7 %collective-permute-start.12 = (f32[2,128]{1,0:T(2,128)S(1)}, f32[2,128]{1,0:T(2,128)S(1)}, u32[]{:S(2)}, u32[]{:S(2)}) collective-permute-start(f32[2,128]{1,0:T(2,128)S(1)} %get-tuple-element.86.refs_0_), channel_id=1, source_target_pairs={{0,2},{1,3},{2,0},{3,1},{4,6},{5,7},{6,4},{7,5},{8,10},{9,11},{10,... | collective-permute-start | bytes 3080 | tf_op jit(solution)/shard_map/ppermute | solution.py:545
  35.7 0.6 %collective-permute-start.11 = (f32[2,128]{1,0:T(2,128)S(1)}, f32[2,128]{1,0:T(2,128)S(1)}, u32[]{:S(2)}, u32[]{:S(2)}) collective-permute-start(f32[2,128]{1,0:T(2,128)S(1)} %get-tuple-element.86.refs_0_), channel_id=1, source_target_pairs={{0,1},{1,0},{2,3},{3,2},{4,5},{5,4},{6,7},{7,6},{8,9},{9,8},{10,11... | collective-permute-start | bytes 3080 | tf_op jit(solution)/shard_map/ppermute | solution.py:545
  36.3 1.1 %collective-permute-done.13.refs_3_ = f32[2,128]{1,0:T(2,128)S(1)} collective-permute-done((f32[2,128]{1,0:T(2,128)S(1)}, f32[2,128]{1,0:T(2,128)S(1)}, u32[]{:S(2)}, u32[]{:S(2)}) %collective-permute-start.13) | collective-permute-done | bytes 1056 | tf_op jit(solution)/shard_map/ppermute | solution.py:545
  37.5 1.1 %collective-permute-done.12.refs_2_ = f32[2,128]{1,0:T(2,128)S(1)} collective-permute-done((f32[2,128]{1,0:T(2,128)S(1)}, f32[2,128]{1,0:T(2,128)S(1)}, u32[]{:S(2)}, u32[]{:S(2)}) %collective-permute-start.12) | collective-permute-done | bytes 1056 | tf_op jit(solution)/shard_map/ppermute | solution.py:545
  38.6 0.0 collective-permute-done.11.refs_1_
  38.6 1.3 %iterate.4 = (f32[8,128,128]{2,1,0:T(8,128)S(1)}, f32[8,128,128]{2,1,0:T(8,128)S(1)}, f32[2,128]{1,0:T(2,128)S(1)}) custom-call(s32[8,88]{1,0:T(8,128)S(4)} %get-tuple-element.60.plan, bf16[2,81,128,128]{3,2,1,0:T(8,128)(2,1)S(1)} %get-tuple-element.80.buf, f32[8,128,128]{2,1,0:T(8,128)S(1)} %get-tuple-element.84.vec_in, ...), custom_call_target="tpu_custom_call" | custom-call | flops 671088640 | bytes 5242880 | tf_op jit(solution)/shard_map/iterate/pallas_call | solution.py:709
  39.9 0.1 collective-permute-start.16
  40.0 0.7 %collective-permute-start.15 = (f32[2,128]{1,0:T(2,128)S(1)}, f32[2,128]{1,0:T(2,128)S(1)}, u32[]{:S(2)}, u32[]{:S(2)}) collective-permute-start(f32[2,128]{1,0:T(2,128)S(1)} %get-tuple-element.89.refs_0_), channel_id=1, source_target_pairs={{0,2},{1,3},{2,0},{3,1},{4,6},{5,7},{6,4},{7,5},{8,10},{9,11},{10,... | collective-permute-start | bytes 3080 | tf_op jit(solution)/shard_map/ppermute | solution.py:545
  40.8 1.1 %collective-permute-start.14 = (f32[2,128]{1,0:T(2,128)S(1)}, f32[2,128]{1,0:T(2,128)S(1)}, u32[]{:S(2)}, u32[]{:S(2)}) collective-permute-start(f32[2,128]{1,0:T(2,128)S(1)} %get-tuple-element.89.refs_0_), channel_id=1, source_target_pairs={{0,1},{1,0},{2,3},{3,2},{4,5},{5,4},{6,7},{7,6},{8,9},{9,8},{10,11... | collective-permute-start | bytes 3080 | tf_op jit(solution)/shard_map/ppermute | solution.py:545
  41.8 1.1 %collective-permute-done.16.refs_3_ = f32[2,128]{1,0:T(2,128)S(1)} collective-permute-done((f32[2,128]{1,0:T(2,128)S(1)}, f32[2,128]{1,0:T(2,128)S(1)}, u32[]{:S(2)}, u32[]{:S(2)}) %collective-permute-start.16) | collective-permute-done | bytes 1056 | tf_op jit(solution)/shard_map/ppermute | solution.py:545
  42.9 0.7 %collective-permute-done.15.refs_2_ = f32[2,128]{1,0:T(2,128)S(1)} collective-permute-done((f32[2,128]{1,0:T(2,128)S(1)}, f32[2,128]{1,0:T(2,128)S(1)}, u32[]{:S(2)}, u32[]{:S(2)}) %collective-permute-start.15) | collective-permute-done | bytes 1056 | tf_op jit(solution)/shard_map/ppermute | solution.py:545
  43.6 0.0 collective-permute-done.14.refs_1_
  43.6 1.3 %iterate.5 = (f32[8,128,128]{2,1,0:T(8,128)S(1)}, f32[8,128,128]{2,1,0:T(8,128)S(1)}, f32[2,128]{1,0:T(2,128)S(1)}) custom-call(s32[8,88]{1,0:T(8,128)S(4)} %get-tuple-element.60.plan, bf16[2,81,128,128]{3,2,1,0:T(8,128)(2,1)S(1)} %get-tuple-element.80.buf, f32[8,128,128]{2,1,0:T(8,128)S(1)} %get-tuple-element.87.vec_in, ...), custom_call_target="tpu_custom_call" | custom-call | flops 671088640 | bytes 5242880 | tf_op jit(solution)/shard_map/iterate/pallas_call | solution.py:709
  44.9 0.6 %collective-permute-start.19 = (f32[2,128]{1,0:T(2,128)S(1)}, f32[2,128]{1,0:T(2,128)S(1)}, u32[]{:S(2)}, u32[]{:S(2)}) collective-permute-start(f32[2,128]{1,0:T(2,128)S(1)} %get-tuple-element.92.refs_0_), channel_id=1, source_target_pairs={{0,3},{1,2},{2,1},{3,0},{4,7},{5,6},{6,5},{7,4},{8,11},{9,10},{10,... | collective-permute-start | bytes 3080 | tf_op jit(solution)/shard_map/ppermute | solution.py:545
  45.5 0.7 %collective-permute-start.18 = (f32[2,128]{1,0:T(2,128)S(1)}, f32[2,128]{1,0:T(2,128)S(1)}, u32[]{:S(2)}, u32[]{:S(2)}) collective-permute-start(f32[2,128]{1,0:T(2,128)S(1)} %get-tuple-element.92.refs_0_), channel_id=1, source_target_pairs={{0,2},{1,3},{2,0},{3,1},{4,6},{5,7},{6,4},{7,5},{8,10},{9,11},{10,... | collective-permute-start | bytes 3080 | tf_op jit(solution)/shard_map/ppermute | solution.py:545
  46.2 0.6 %collective-permute-start.17 = (f32[2,128]{1,0:T(2,128)S(1)}, f32[2,128]{1,0:T(2,128)S(1)}, u32[]{:S(2)}, u32[]{:S(2)}) collective-permute-start(f32[2,128]{1,0:T(2,128)S(1)} %get-tuple-element.92.refs_0_), channel_id=1, source_target_pairs={{0,1},{1,0},{2,3},{3,2},{4,5},{5,4},{6,7},{7,6},{8,9},{9,8},{10,11... | collective-permute-start | bytes 3080 | tf_op jit(solution)/shard_map/ppermute | solution.py:545
  46.9 1.1 %collective-permute-done.19.refs_3_ = f32[2,128]{1,0:T(2,128)S(1)} collective-permute-done((f32[2,128]{1,0:T(2,128)S(1)}, f32[2,128]{1,0:T(2,128)S(1)}, u32[]{:S(2)}, u32[]{:S(2)}) %collective-permute-start.19) | collective-permute-done | bytes 1056 | tf_op jit(solution)/shard_map/ppermute | solution.py:545
  48.0 1.1 %collective-permute-done.18.refs_2_ = f32[2,128]{1,0:T(2,128)S(1)} collective-permute-done((f32[2,128]{1,0:T(2,128)S(1)}, f32[2,128]{1,0:T(2,128)S(1)}, u32[]{:S(2)}, u32[]{:S(2)}) %collective-permute-start.18) | collective-permute-done | bytes 1056 | tf_op jit(solution)/shard_map/ppermute | solution.py:545
  49.1 0.0 collective-permute-done.17.refs_1_
  49.1 0.4 last.1
  49.5 0.0 copy-start.2
  49.5 0.1 collective-permute-start.22
  49.6 0.7 %collective-permute-start.21 = (f32[2,128]{1,0:T(2,128)S(1)}, f32[2,128]{1,0:T(2,128)S(1)}, u32[]{:S(2)}, u32[]{:S(2)}) collective-permute-start(f32[2,128]{1,0:T(2,128)S(1)} %get-tuple-element.94.refs_0_), channel_id=1, source_target_pairs={{0,2},{1,3},{2,0},{3,1},{4,6},{5,7},{6,4},{7,5},{8,10},{9,11},{10,... | collective-permute-start | bytes 3080 | tf_op jit(solution)/shard_map/ppermute | solution.py:545
  50.3 1.1 %collective-permute-start.20 = (f32[2,128]{1,0:T(2,128)S(1)}, f32[2,128]{1,0:T(2,128)S(1)}, u32[]{:S(2)}, u32[]{:S(2)}) collective-permute-start(f32[2,128]{1,0:T(2,128)S(1)} %get-tuple-element.94.refs_0_), channel_id=1, source_target_pairs={{0,1},{1,0},{2,3},{3,2},{4,5},{5,4},{6,7},{7,6},{8,9},{9,8},{10,11... | collective-permute-start | bytes 3080 | tf_op jit(solution)/shard_map/ppermute | solution.py:545
  51.4 0.2 turn.1.vec
  51.6 0.9 %collective-permute-done.22.refs_3_ = f32[2,128]{1,0:T(2,128)S(1)} collective-permute-done((f32[2,128]{1,0:T(2,128)S(1)}, f32[2,128]{1,0:T(2,128)S(1)}, u32[]{:S(2)}, u32[]{:S(2)}) %collective-permute-start.22) | collective-permute-done | bytes 1056 | tf_op jit(solution)/shard_map/ppermute | solution.py:545
  52.5 0.7 %collective-permute-done.21.refs_2_ = f32[2,128]{1,0:T(2,128)S(1)} collective-permute-done((f32[2,128]{1,0:T(2,128)S(1)}, f32[2,128]{1,0:T(2,128)S(1)}, u32[]{:S(2)}, u32[]{:S(2)}) %collective-permute-start.21) | collective-permute-done | bytes 1056 | tf_op jit(solution)/shard_map/ppermute | solution.py:545
  53.2 0.0 collective-permute-done.20.refs_1_
  53.2 0.9 %psi.1 = bf16[8,128,128]{2,1,0:T(8,128)(2,1)} custom-call(s32[8,88]{1,0:T(8,128)S(4)} %get-tuple-element.60.plan, f32[8,128,128]{2,1,0:T(8,128)S(1)} %turn.1.vec, f32[2,128]{1,0:T(2,128)S(1)} %get-tuple-element.94.refs_0_, f32[2,128]{1,0:T(2,128)S(1)} %collective-permute-done.20.refs_1_, f32[2,128]{1,0:T(2,128)S(1)} %collective-permute-done.21.refs_2_, ...), custom_call_target="tpu_custom_call" | custom-call | bytes 524288 | tf_op jit(solution)/shard_map/psi/pallas_call | solution.py:740
  54.1 0.0 copy-done.2
  (4 shorter events, 0.0 us)
Async XLA Ops:
  0.6 12.0 %collective-permute-start.2 = (bf16[8,128,128]{2,1,0:T(8,128)(2,1)}, bf16[8,128,128]{2,1,0:T(8,128)(2,1)}, u32[]{:S(2)}, u32[]{:S(2)}) collective-permute-start(bf16[8,128,128]{2,1,0:T(8,128)(2,1)} %bitcast.8), channel_id=1, source_target_pairs={{0,4},{4,0},{8,12},{12,8},{1,5},{5,1},{9,13},{13,9},{2,6},{6,2},{1... | collective-permute-start | bytes 786440 | tf_op jit(solution)/shard_map/ppermute | solution.py:545
  3.7 8.9 %collective-permute-start.4 = (f32[8,128]{1,0:T(8,128)}, f32[8,128]{1,0:T(8,128)S(1)}, u32[]{:S(2)}, u32[]{:S(2)}) collective-permute-start(f32[8,128]{1,0:T(8,128)} %bitcast.10), channel_id=1, source_target_pairs={{0,12},{4,8},{8,4},{12,0},{1,13},{5,9},{9,5},{13,1},{2,14},{6,10},... | collective-permute-start | bytes 12296 | tf_op jit(solution)/shard_map/ppermute | solution.py:545
  6.2 6.5 %collective-permute-start.3 = (f32[8,128]{1,0:T(8,128)}, f32[8,128]{1,0:T(8,128)S(1)}, u32[]{:S(2)}, u32[]{:S(2)}) collective-permute-start(f32[8,128]{1,0:T(8,128)} %bitcast.11), channel_id=1, source_target_pairs={{0,8},{4,12},{8,0},{12,4},{1,9},{5,13},{9,1},{13,5},{2,10},{6,14},... | collective-permute-start | bytes 12296 | tf_op jit(solution)/shard_map/ppermute | solution.py:545
  8.8 3.9 %copy-start.3 = (bf16[1568,128]{1,0:T(8,128)(2,1)}, bf16[1568,128]{1,0:T(8,128)(2,1)S(1)}, u32[]{:S(2)}) copy-start(bf16[1568,128]{1,0:T(8,128)(2,1)S(1)} %get-tuple-element.72.refs_1_) | copy-start | bytes 1204228
  8.8 12.5 %collective-permute-start.5 = (bf16[1600,128]{1,0:T(8,128)(2,1)S(1)}, bf16[1600,128]{1,0:T(8,128)(2,1)S(1)}, u32[]{:S(2)}, u32[]{:S(2)}) collective-permute-start(bf16[1600,128]{1,0:T(8,128)(2,1)S(1)} %get-tuple-element.62), channel_id=1, source_target_pairs={{0,4},{4,0},{8,12},{12,8},{1,5},{5,1},{9,13},{13,9},{2,6},{6,2},{1... | collective-permute-start | bytes 1228808 | tf_op jit(solution)/shard_map/ppermute | solution.py:545
  12.7 0.6 %copy-start.4 = (f32[8,128]{1,0:T(8,128)}, f32[8,128]{1,0:T(8,128)S(1)}, u32[]{:S(2)}) copy-start(f32[8,128]{1,0:T(8,128)S(1)} %collective-permute-done.4.refs_2_.refs_4_) | copy-start | bytes 12292
  12.7 0.6 %copy-start.5 = (f32[8,128]{1,0:T(8,128)}, f32[8,128]{1,0:T(8,128)S(1)}, u32[]{:S(2)}) copy-start(f32[8,128]{1,0:T(8,128)S(1)} %collective-permute-done.3.refs_1_.refs_3_) | copy-start | bytes 12292
  13.3 2.4 %copy-start = (bf16[1,8,128,128]{3,2,1,0:T(8,128)(2,1)S(1)}, bf16[1,8,128,128]{3,2,1,0:T(8,128)(2,1)}, u32[]{:S(2)}) copy-start(bf16[1,8,128,128]{3,2,1,0:T(8,128)(2,1)} %param.10) | copy-start | bytes 786436
  13.3 2.4 %copy-start.1 = (f32[1,8,128]{2,1,0:T(8,128)S(1)}, f32[1,8,128]{2,1,0:T(8,128)}, u32[]{:S(2)}) copy-start(f32[1,8,128]{2,1,0:T(8,128)} %param.11) | copy-start | bytes 12292
  13.6 13.2 %collective-permute-start.7 = (bf16[1040,128]{1,0:T(8,128)(2,1)S(1)}, bf16[1040,128]{1,0:T(8,128)(2,1)S(1)}, u32[]{:S(2)}, u32[]{:S(2)}) collective-permute-start(bf16[1040,128]{1,0:T(8,128)(2,1)S(1)} %get-tuple-element.74), channel_id=1, source_target_pairs={{0,4},{4,0},{8,12},{12,8},{1,5},{5,1},{9,13},{13,9},{2,6},{6,2},{1... | collective-permute-start | bytes 798728 | tf_op jit(solution)/shard_map/ppermute | solution.py:545
  14.1 14.1 %collective-permute-start.6 = (bf16[528,128]{1,0:T(8,128)(2,1)S(1)}, bf16[528,128]{1,0:T(8,128)(2,1)S(1)}, u32[]{:S(2)}, u32[]{:S(2)}) collective-permute-start(bf16[528,128]{1,0:T(8,128)(2,1)S(1)} %get-tuple-element.73), channel_id=1, source_target_pairs={{0,4},{4,0},{8,12},{12,8},{1,5},{5,1},{9,13},{13,9},{2,6},{6,2},{1... | collective-permute-start | bytes 405512 | tf_op jit(solution)/shard_map/ppermute | solution.py:545
  29.4 3.1 %collective-permute-start.10 = (f32[2,128]{1,0:T(2,128)S(1)}, f32[2,128]{1,0:T(2,128)S(1)}, u32[]{:S(2)}, u32[]{:S(2)}) collective-permute-start(f32[2,128]{1,0:T(2,128)S(1)} %get-tuple-element.83.refs_0_), channel_id=1, source_target_pairs={{0,3},{1,2},{2,1},{3,0},{4,7},{5,6},{6,5},{7,4},{8,11},{9,10},{10,... | collective-permute-start | bytes 3080 | tf_op jit(solution)/shard_map/ppermute | solution.py:545
  29.4 3.6 %collective-permute-start.9 = (f32[2,128]{1,0:T(2,128)S(1)}, f32[2,128]{1,0:T(2,128)S(1)}, u32[]{:S(2)}, u32[]{:S(2)}) collective-permute-start(f32[2,128]{1,0:T(2,128)S(1)} %get-tuple-element.83.refs_0_), channel_id=1, source_target_pairs={{0,2},{1,3},{2,0},{3,1},{4,6},{5,7},{6,4},{7,5},{8,10},{9,11},{10,... | collective-permute-start | bytes 3080 | tf_op jit(solution)/shard_map/ppermute | solution.py:545
  30.2 2.8 %collective-permute-start.8 = (f32[2,128]{1,0:T(2,128)S(1)}, f32[2,128]{1,0:T(2,128)S(1)}, u32[]{:S(2)}, u32[]{:S(2)}) collective-permute-start(f32[2,128]{1,0:T(2,128)S(1)} %get-tuple-element.83.refs_0_), channel_id=1, source_target_pairs={{0,1},{1,0},{2,3},{3,2},{4,5},{5,4},{6,7},{7,6},{8,9},{9,8},{10,11... | collective-permute-start | bytes 3080 | tf_op jit(solution)/shard_map/ppermute | solution.py:545
  34.4 3.1 %collective-permute-start.13 = (f32[2,128]{1,0:T(2,128)S(1)}, f32[2,128]{1,0:T(2,128)S(1)}, u32[]{:S(2)}, u32[]{:S(2)}) collective-permute-start(f32[2,128]{1,0:T(2,128)S(1)} %get-tuple-element.86.refs_0_), channel_id=1, source_target_pairs={{0,3},{1,2},{2,1},{3,0},{4,7},{5,6},{6,5},{7,4},{8,11},{9,10},{10,... | collective-permute-start | bytes 3080 | tf_op jit(solution)/shard_map/ppermute | solution.py:545
  35.0 3.6 %collective-permute-start.12 = (f32[2,128]{1,0:T(2,128)S(1)}, f32[2,128]{1,0:T(2,128)S(1)}, u32[]{:S(2)}, u32[]{:S(2)}) collective-permute-start(f32[2,128]{1,0:T(2,128)S(1)} %get-tuple-element.86.refs_0_), channel_id=1, source_target_pairs={{0,2},{1,3},{2,0},{3,1},{4,6},{5,7},{6,4},{7,5},{8,10},{9,11},{10,... | collective-permute-start | bytes 3080 | tf_op jit(solution)/shard_map/ppermute | solution.py:545
  35.7 2.8 %collective-permute-start.11 = (f32[2,128]{1,0:T(2,128)S(1)}, f32[2,128]{1,0:T(2,128)S(1)}, u32[]{:S(2)}, u32[]{:S(2)}) collective-permute-start(f32[2,128]{1,0:T(2,128)S(1)} %get-tuple-element.86.refs_0_), channel_id=1, source_target_pairs={{0,1},{1,0},{2,3},{3,2},{4,5},{5,4},{6,7},{7,6},{8,9},{9,8},{10,11... | collective-permute-start | bytes 3080 | tf_op jit(solution)/shard_map/ppermute | solution.py:545
  39.9 3.1 %collective-permute-start.16 = (f32[2,128]{1,0:T(2,128)S(1)}, f32[2,128]{1,0:T(2,128)S(1)}, u32[]{:S(2)}, u32[]{:S(2)}) collective-permute-start(f32[2,128]{1,0:T(2,128)S(1)} %get-tuple-element.89.refs_0_), channel_id=1, source_target_pairs={{0,3},{1,2},{2,1},{3,0},{4,7},{5,6},{6,5},{7,4},{8,11},{9,10},{10,... | collective-permute-start | bytes 3080 | tf_op jit(solution)/shard_map/ppermute | solution.py:545
  40.0 3.6 %collective-permute-start.15 = (f32[2,128]{1,0:T(2,128)S(1)}, f32[2,128]{1,0:T(2,128)S(1)}, u32[]{:S(2)}, u32[]{:S(2)}) collective-permute-start(f32[2,128]{1,0:T(2,128)S(1)} %get-tuple-element.89.refs_0_), channel_id=1, source_target_pairs={{0,2},{1,3},{2,0},{3,1},{4,6},{5,7},{6,4},{7,5},{8,10},{9,11},{10,... | collective-permute-start | bytes 3080 | tf_op jit(solution)/shard_map/ppermute | solution.py:545
  40.8 2.8 %collective-permute-start.14 = (f32[2,128]{1,0:T(2,128)S(1)}, f32[2,128]{1,0:T(2,128)S(1)}, u32[]{:S(2)}, u32[]{:S(2)}) collective-permute-start(f32[2,128]{1,0:T(2,128)S(1)} %get-tuple-element.89.refs_0_), channel_id=1, source_target_pairs={{0,1},{1,0},{2,3},{3,2},{4,5},{5,4},{6,7},{7,6},{8,9},{9,8},{10,11... | collective-permute-start | bytes 3080 | tf_op jit(solution)/shard_map/ppermute | solution.py:545
  44.9 3.1 %collective-permute-start.19 = (f32[2,128]{1,0:T(2,128)S(1)}, f32[2,128]{1,0:T(2,128)S(1)}, u32[]{:S(2)}, u32[]{:S(2)}) collective-permute-start(f32[2,128]{1,0:T(2,128)S(1)} %get-tuple-element.92.refs_0_), channel_id=1, source_target_pairs={{0,3},{1,2},{2,1},{3,0},{4,7},{5,6},{6,5},{7,4},{8,11},{9,10},{10,... | collective-permute-start | bytes 3080 | tf_op jit(solution)/shard_map/ppermute | solution.py:545
  45.5 3.6 %collective-permute-start.18 = (f32[2,128]{1,0:T(2,128)S(1)}, f32[2,128]{1,0:T(2,128)S(1)}, u32[]{:S(2)}, u32[]{:S(2)}) collective-permute-start(f32[2,128]{1,0:T(2,128)S(1)} %get-tuple-element.92.refs_0_), channel_id=1, source_target_pairs={{0,2},{1,3},{2,0},{3,1},{4,6},{5,7},{6,4},{7,5},{8,10},{9,11},{10,... | collective-permute-start | bytes 3080 | tf_op jit(solution)/shard_map/ppermute | solution.py:545
  46.2 2.8 %collective-permute-start.17 = (f32[2,128]{1,0:T(2,128)S(1)}, f32[2,128]{1,0:T(2,128)S(1)}, u32[]{:S(2)}, u32[]{:S(2)}) collective-permute-start(f32[2,128]{1,0:T(2,128)S(1)} %get-tuple-element.92.refs_0_), channel_id=1, source_target_pairs={{0,1},{1,0},{2,3},{3,2},{4,5},{5,4},{6,7},{7,6},{8,9},{9,8},{10,11... | collective-permute-start | bytes 3080 | tf_op jit(solution)/shard_map/ppermute | solution.py:545
  49.5 4.6 %copy-start.2 = (f32[1,128]{1,0:T(1,128)}, f32[1,128]{1,0:T(1,128)S(1)}, u32[]{:S(2)}) copy-start(f32[1,128]{1,0:T(1,128)S(1)} %get-tuple-element.95) | copy-start | bytes 1540
  49.5 3.1 %collective-permute-start.22 = (f32[2,128]{1,0:T(2,128)S(1)}, f32[2,128]{1,0:T(2,128)S(1)}, u32[]{:S(2)}, u32[]{:S(2)}) collective-permute-start(f32[2,128]{1,0:T(2,128)S(1)} %get-tuple-element.94.refs_0_), channel_id=1, source_target_pairs={{0,3},{1,2},{2,1},{3,0},{4,7},{5,6},{6,5},{7,4},{8,11},{9,10},{10,... | collective-permute-start | bytes 3080 | tf_op jit(solution)/shard_map/ppermute | solution.py:545
  49.6 3.6 %collective-permute-start.21 = (f32[2,128]{1,0:T(2,128)S(1)}, f32[2,128]{1,0:T(2,128)S(1)}, u32[]{:S(2)}, u32[]{:S(2)}) collective-permute-start(f32[2,128]{1,0:T(2,128)S(1)} %get-tuple-element.94.refs_0_), channel_id=1, source_target_pairs={{0,2},{1,3},{2,0},{3,1},{4,6},{5,7},{6,4},{7,5},{8,10},{9,11},{10,... | collective-permute-start | bytes 3080 | tf_op jit(solution)/shard_map/ppermute | solution.py:545
  50.3 2.8 %collective-permute-start.20 = (f32[2,128]{1,0:T(2,128)S(1)}, f32[2,128]{1,0:T(2,128)S(1)}, u32[]{:S(2)}, u32[]{:S(2)}) collective-permute-start(f32[2,128]{1,0:T(2,128)S(1)} %get-tuple-element.94.refs_0_), channel_id=1, source_target_pairs={{0,1},{1,0},{2,3},{3,2},{4,5},{5,4},{6,7},{7,6},{8,9},{9,8},{10,11... | collective-permute-start | bytes 3080 | tf_op jit(solution)/shard_map/ppermute | solution.py:545
where the time goes:
time: 54.4 us; the launch traced here: 54.2 us
  starting transfers between devices  19.3 us (35%)
  waiting for transfers between devices  18.6 us (34%)
  Pallas kernels  14.8 us (27%)
  between operations  0.96 us (2%)
  local copies, waits for them, and re-layouts  0.59 us (1%)
    ppermute x21, starting transfers between devices, swapped(): return lax.ppermute(value, axis, [(k, k ^ mask) for k in range(size)])  19.3 us
    ppermute x21, waiting for transfers between devices, swapped(): return lax.ppermute(value, axis, [(k, k ^ mask) for k in range(size)])  18.6 us
    pallas_call x3, Pallas kernels, local(): pl.pallas_call(functools.partial(iter_kernel, count, tensor), out_shape=[...  3.97 us
    pallas_call x1, Pallas kernels, local(): pl.pallas_call(functools.partial(own_kernel, group, chans), out_shape=[bu...  3.18 us
    pallas_call x1, Pallas kernels, local(): pl.pallas_call(functools.partial(pack_kernel, cuts[0], cuts[usual:], grou...  2.43 us
    pallas_call x1, Pallas kernels, local(): pl.pallas_call(functools.partial(mid_kernel, cuts[1], group), out_shape=[...  1.48 us
  transfers between devices with their start and end apart: 21, of which 13 were waited for; matrix products, arithmetic and copies ran while one was open for 0% of the time, Pallas kernels for 16%

commit v1 on v0

--- a/solution.py
+++ b/solution.py
@@ -9,6 +9,7 @@
 
 ITERS = 4
 STEP_SIZE = 0.5
+EARLY = 3
 PACK_COST = 10**7
 REST_COST = 10**10
 OWN_COST = 0
@@ -106,7 +107,6 @@
     out_hbm, table, flag, env, out, spare, mask_ref, ranks_ref, weight_ref, rows_ref = refs[:10]
     scalar_sems, sems, out_sems, over_sem = refs[10:]
     sectors, chans = mask_ref.shape
-    blocks = sectors * chans
     scalars = [
         pltpu.make_async_copy(mask_hbm, mask_ref, scalar_sems.at[0]),
         pltpu.make_async_copy(ranks_hbm, ranks_ref, scalar_sems.at[1]),
@@ -119,28 +119,24 @@
         part = pl.ds(s * chans, chans)
         return pltpu.make_async_copy(env_hbm.at[part], env.at[part], sems.at[s])
 
-    for s in range(sectors):
+    for s in range(min(EARLY, sectors)):
         fetch(s).start()
-    for c in scalars:
-        c.wait()
+    scalars[0].wait()
+    for s in range(EARLY, sectors):
+        fetch(s).start()
     n = jnp.int32(0)
     for s in range(sectors):
-        table[RANK, s] = ranks_ref[s]
         k = jnp.int32(0)
         for w in range(chans):
             m = mask_ref[s, w]
             table[SOURCE, n] = jnp.int32(s * chans + w)
             table[SECTOR, n] = jnp.int32(s)
-            table[PLACE, n] = k
-            table[TARGET, n] = s * chans + k
             n = n + m
             k = k + m
         table[COUNT, s] = k
     for d in range(2 * group):
         table[SOURCE, n + d] = jnp.int32(0)
         table[SECTOR, n + d] = jnp.int32(0)
-        table[PLACE, n + d] = jnp.int32(chans)
-        table[TARGET, n + d] = jnp.int32(blocks)
     table[NUMBER, 0] = n
     flag[0] = n
 
@@ -154,6 +150,10 @@
         lax.fori_loop(here, need, wait, 0)
         return need
 
+    for c in scalars[1:]:
+        c.wait()
+    for s in range(sectors):
+        table[RANK, s] = ranks_ref[s]
     extra = weight_rows(sectors)
     edge = env.shape[-1]
     size = (cut[1] - cut[0]) * edge
@@ -272,8 +272,10 @@
         plan[END, places[s]] = start
 
     def rest(k, carry):
-        for row in (SOURCE, SECTOR, PLACE, TARGET):
-            plan[row, k] = table[row, k]
+        plan[SOURCE, k] = jnp.int32(0)
+        plan[SECTOR, k] = jnp.int32(0)
+        plan[PLACE, k] = jnp.int32(chans)
+        plan[TARGET, k] = jnp.int32(sectors * chans)
         return carry
 
     lax.fori_loop(n, n + table.shape[1] - sectors * chans, rest, 0)

time: 54.4 us -> 54.8 us (level)
  Pallas kernels: 14.8 us -> 15.4 us
where the time goes in v1:
time: 54.8 us; the launch traced here: 55 us
  starting transfers between devices  19.3 us (35%)
  waiting for transfers between devices  18.8 us (34%)
  Pallas kernels  15.4 us (28%)
  between operations  0.96 us (2%)
  local copies, waits for them, and re-layouts  0.59 us (1%)
    ppermute x21, starting transfers between devices, swapped(): return lax.ppermute(value, axis, [(k, k ^ mask) for k in range(size)])  19.3 us
    ppermute x21, waiting for transfers between devices, swapped(): return lax.ppermute(value, axis, [(k, k ^ mask) for k in range(size)])  18.8 us
    pallas_call x3, Pallas kernels, local(): pl.pallas_call(functools.partial(iter_kernel, count, tensor), out_shape=[...  3.97 us
    pallas_call x1, Pallas kernels, local(): pl.pallas_call(functools.partial(own_kernel, group, chans), out_shape=[bu...  3.18 us
    pallas_call x1, Pallas kernels, local(): pl.pallas_call(functools.partial(pack_kernel, cuts[0], cuts[usual:], grou...  2.52 us
    pallas_call x1, Pallas kernels, local(): pl.pallas_call(functools.partial(first_kernel, cuts[usual - 1:], group),...  1.52 us
    pallas_call x1, Pallas kernels, local(): pl.pallas_call(functools.partial(mid_kernel, cuts[1], group), out_shape=[...  1.48 us
  transfers between devices with their start and end apart: 21, of which 13 were waited for; matrix products, arithmetic and copies ran while one was open for 0% of the time, Pallas kernels for 16%

profile of v1, /device:TPU:0, one launch (start us, length us, event | category | flops | bytes accessed | tf_op | source)
XLA Modules:
  0.0 55.0 jit_solution(3877173489708331242)
XLA Ops:
  0.6 3.1 %collective-permute-start.2 = (bf16[8,128,128]{2,1,0:T(8,128)(2,1)}, bf16[8,128,128]{2,1,0:T(8,128)(2,1)}, u32[]{:S(2)}, u32[]{:S(2)}) collective-permute-start(bf16[8,128,128]{2,1,0:T(8,128)(2,1)} %bitcast.8), channel_id=1, source_target_pairs={{0,4},{4,0},{8,12},{12,8},{1,5},{5,1},{9,13},{13,9},{2,6},{6,2},{1... | collective-permute-start | bytes 786440 | tf_op jit(solution)/shard_map/ppermute | solution.py:547
  3.7 2.5 %collective-permute-start.4 = (f32[8,128]{1,0:T(8,128)}, f32[8,128]{1,0:T(8,128)S(1)}, u32[]{:S(2)}, u32[]{:S(2)}) collective-permute-start(f32[8,128]{1,0:T(8,128)} %bitcast.10), channel_id=1, source_target_pairs={{0,12},{4,8},{8,4},{12,0},{1,13},{5,9},{9,5},{13,1},{2,14},{6,10},... | collective-permute-start | bytes 12296 | tf_op jit(solution)/shard_map/ppermute | solution.py:547
  6.2 0.1 collective-permute-start.3
  6.3 2.5 %pack.1 = (bf16[528,128]{1,0:T(8,128)(2,1)}, bf16[1568,128]{1,0:T(8,128)(2,1)S(1)}, bf16[1600,128]{1,0:T(8,128)(2,1)S(1)}, s32[8,88]{1,0:T(8,128)S(4)}, s32[1]{0:T(128)S(4)}, /*index=5*/bf16[80,128,128]{2,1,0:T(8,128)(2,1)S(1)}) custom-call(s32[8,10]{1,0:T(8,128)} %mask_hbm.1, s32[8]{0:T(128)} %ranks_hbm.1, f32[8,128]{1,0:T(8,128)} %bitcast.12, ...), custom_call_target="tpu_custom_call" | custom-call | flops 10000000 | bytes 5242880 | tf_op jit(solution)/shard_map/pack/pallas_call | solution.py:588
  8.9 0.0 copy-start.3
  8.9 1.9 %collective-permute-start.5 = (bf16[1600,128]{1,0:T(8,128)(2,1)S(1)}, bf16[1600,128]{1,0:T(8,128)(2,1)S(1)}, u32[]{:S(2)}, u32[]{:S(2)}) collective-permute-start(bf16[1600,128]{1,0:T(8,128)(2,1)S(1)} %get-tuple-element.62), channel_id=1, source_target_pairs={{0,4},{4,0},{8,12},{12,8},{1,5},{5,1},{9,13},{13,9},{2,6},{6,2},{1... | collective-permute-start | bytes 1228808 | tf_op jit(solution)/shard_map/ppermute | solution.py:547
  10.7 1.9 %collective-permute-done.4.refs_2_.refs_4_ = f32[8,128]{1,0:T(8,128)S(1)} collective-permute-done((f32[8,128]{1,0:T(8,128)}, f32[8,128]{1,0:T(8,128)S(1)}, u32[]{:S(2)}, u32[]{:S(2)}) %collective-permute-start.4) | collective-permute-done | bytes 4128 | tf_op jit(solution)/shard_map/ppermute | solution.py:547
  12.7 0.0 copy-start.4
  12.7 0.0 collective-permute-done.3.refs_1_.refs_3_
  12.7 0.0 collective-permute-done.2.other_site.refs_2_
  12.7 0.0 copy-done.3
  12.7 0.6 %copy-done.4 = f32[8,128]{1,0:T(8,128)} copy-done((f32[8,128]{1,0:T(8,128)}, f32[8,128]{1,0:T(8,128)S(1)}, u32[]{:S(2)}) %copy-start.4) | copy-done | bytes 4120
  13.2 0.0 copy-done.5
  13.3 0.3 rest.1
  13.6 0.6 collective-permute-start.7
  14.1 1.5 %collective-permute-start.6 = (bf16[528,128]{1,0:T(8,128)(2,1)S(1)}, bf16[528,128]{1,0:T(8,128)(2,1)S(1)}, u32[]{:S(2)}, u32[]{:S(2)}) collective-permute-start(bf16[528,128]{1,0:T(8,128)(2,1)S(1)} %get-tuple-element.73), channel_id=1, source_target_pairs={{0,4},{4,0},{8,12},{12,8},{1,5},{5,1},{9,13},{13,9},{2,6},{6,2},{1... | collective-permute-start | bytes 405512 | tf_op jit(solution)/shard_map/ppermute | solution.py:547
  15.7 0.0 copy-done
  15.7 0.0 copy-done.1
  15.7 3.2 %own.1 = (bf16[2,81,128,128]{3,2,1,0:T(8,128)(2,1)S(1)}, f32[2,8,16,128]{3,2,1,0:T(8,128)S(1)}, f32[8,128]{1,0:T(8,128)S(1)}, f32[8,128,128]{2,1,0:T(8,128)S(1)}, s32[8,88]{1,0:T(8,128)S(4)}) custom-call(s32[8,88]{1,0:T(8,128)S(4)} %get-tuple-element.58.table, bf16[80,128,128]{2,1,0:T(8,128)(2,1)S(1)} %get-tuple-element.59.env, ...), custom_call_target="tpu_custom_call" | custom-call | tf_op jit(solution)/shard_map/own/pallas_call | solution.py:646
  18.9 2.5 %collective-permute-done.5.chunk = bf16[1600,128]{1,0:T(8,128)(2,1)S(1)} collective-permute-done((bf16[1600,128]{1,0:T(8,128)(2,1)S(1)}, bf16[1600,128]{1,0:T(8,128)(2,1)S(1)}, u32[]{:S(2)}, u32[]{:S(2)}) %collective-permute-start.5) | collective-permute-done | bytes 409632 | tf_op jit(solution)/shard_map/ppermute | solution.py:547
  21.4 0.7 %outer.1 = (bf16[2,81,128,128]{3,2,1,0:T(8,128)(2,1)S(1)}, f32[2,8,16,128]{3,2,1,0:T(8,128)S(1)}, f32[8,128,128]{2,1,0:T(8,128)S(1)}, f32[8,128]{1,0:T(8,128)S(1)}) custom-call(s32[8,88]{1,0:T(8,128)S(4)} %get-tuple-element.60.plan, f32[8,128]{1,0:T(8,128)S(1)} %get-tuple-element.61.prefix, ...), custom_call_target="tpu_custom_call", output_to_operand_aliasing={{0}: (3, {}), {1}: (4, {})} | custom-call | tf_op jit(solution)/shard_map/outer/pallas_call | solution.py:658
  22.1 4.8 %collective-permute-done.7.chunk = bf16[1040,128]{1,0:T(8,128)(2,1)S(1)} collective-permute-done((bf16[1040,128]{1,0:T(8,128)(2,1)S(1)}, bf16[1040,128]{1,0:T(8,128)(2,1)S(1)}, u32[]{:S(2)}, u32[]{:S(2)}) %collective-permute-start.7) | collective-permute-done | bytes 266272 | tf_op jit(solution)/shard_map/ppermute | solution.py:547
  26.9 1.5 %mid.1 = (bf16[2,81,128,128]{3,2,1,0:T(8,128)(2,1)S(1)}, f32[2,8,16,128]{3,2,1,0:T(8,128)S(1)}, f32[8,128,128]{2,1,0:T(8,128)S(1)}) custom-call(s32[8,88]{1,0:T(8,128)S(4)} %get-tuple-element.60.plan, f32[8,128,128]{2,1,0:T(8,128)S(1)} %get-tuple-element.65.outer, ...), custom_call_target="tpu_custom_call", output_to_operand_aliasing={{0}: (5, {}), {1}: (6, {})} | custom-call | tf_op jit(solution)/shard_map/mid/pallas_call | solution.py:670
  28.4 0.0 collective-permute-done.6.chunk
  28.4 1.5 %first.1 = (bf16[2,81,128,128]{3,2,1,0:T(8,128)(2,1)S(1)}, f32[2,8,16,128]{3,2,1,0:T(8,128)S(1)}, f32[8,128,128]{2,1,0:T(8,128)S(1)}, f32[2,128]{1,0:T(2,128)S(1)}) custom-call(s32[8,88]{1,0:T(8,128)S(4)} %get-tuple-element.60.plan, f32[8,128,128]{2,1,0:T(8,128)S(1)} %get-tuple-element.65.outer, ...), custom_call_target="tpu_custom_call", output_to_operand_aliasing={{0}: (7, {}), {1}: (8, {}), {2}: (9, {})} | custom-call | flops 671088640 | bytes 5242880 | tf_op jit(solution)/shard_map/first/pallas_call | solution.py:683
  29.9 0.1 collective-permute-start.10
  30.0 0.3 collective-permute-start.9
  30.3 1.5 %collective-permute-start.8 = (f32[2,128]{1,0:T(2,128)S(1)}, f32[2,128]{1,0:T(2,128)S(1)}, u32[]{:S(2)}, u32[]{:S(2)}) collective-permute-start(f32[2,128]{1,0:T(2,128)S(1)} %get-tuple-element.83.refs_0_), channel_id=1, source_target_pairs={{0,1},{1,0},{2,3},{3,2},{4,5},{5,4},{6,7},{7,6},{8,9},{9,8},{10,11... | collective-permute-start | bytes 3080 | tf_op jit(solution)/shard_map/ppermute | solution.py:547
  31.8 0.3 diagonal.1.dh
  32.1 0.9 %collective-permute-done.10.refs_3_ = f32[2,128]{1,0:T(2,128)S(1)} collective-permute-done((f32[2,128]{1,0:T(2,128)S(1)}, f32[2,128]{1,0:T(2,128)S(1)}, u32[]{:S(2)}, u32[]{:S(2)}) %collective-permute-start.10) | collective-permute-done | bytes 1056 | tf_op jit(solution)/shard_map/ppermute | solution.py:547
  33.0 0.6 %collective-permute-done.9.refs_2_ = f32[2,128]{1,0:T(2,128)S(1)} collective-permute-done((f32[2,128]{1,0:T(2,128)S(1)}, f32[2,128]{1,0:T(2,128)S(1)}, u32[]{:S(2)}, u32[]{:S(2)}) %collective-permute-start.9) | collective-permute-done | bytes 1056 | tf_op jit(solution)/shard_map/ppermute | solution.py:547
  33.6 0.0 collective-permute-done.8.refs_1_
  33.6 1.3 %iterate.3 = (f32[8,128,128]{2,1,0:T(8,128)S(1)}, f32[8,128,128]{2,1,0:T(8,128)S(1)}, f32[2,128]{1,0:T(2,128)S(1)}) custom-call(s32[8,88]{1,0:T(8,128)S(4)} %get-tuple-element.60.plan, bf16[2,81,128,128]{3,2,1,0:T(8,128)(2,1)S(1)} %get-tuple-element.80.buf, f32[8,128,128]{2,1,0:T(8,128)S(1)} %get-tuple-element.67.vec.vec_in, ...), custom_call_target="tpu_custom_call" | custom-call | flops 671088640 | bytes 5242880 | tf_op jit(solution)/shard_map/iterate/pallas_call | solution.py:711
  34.9 0.6 %collective-permute-start.13 = (f32[2,128]{1,0:T(2,128)S(1)}, f32[2,128]{1,0:T(2,128)S(1)}, u32[]{:S(2)}, u32[]{:S(2)}) collective-permute-start(f32[2,128]{1,0:T(2,128)S(1)} %get-tuple-element.86.refs_0_), channel_id=1, source_target_pairs={{0,3},{1,2},{2,1},{3,0},{4,7},{5,6},{6,5},{7,4},{8,11},{9,10},{10,... | collective-permute-start | bytes 3080 | tf_op jit(solution)/shard_map/ppermute | solution.py:547
  35.5 0.6 %collective-permute-start.12 = (f32[2,128]{1,0:T(2,128)S(1)}, f32[2,128]{1,0:T(2,128)S(1)}, u32[]{:S(2)}, u32[]{:S(2)}) collective-permute-start(f32[2,128]{1,0:T(2,128)S(1)} %get-tuple-element.86.refs_0_), channel_id=1, source_target_pairs={{0,2},{1,3},{2,0},{3,1},{4,6},{5,7},{6,4},{7,5},{8,10},{9,11},{10,... | collective-permute-start | bytes 3080 | tf_op jit(solution)/shard_map/ppermute | solution.py:547
  36.1 0.8 %collective-permute-start.11 = (f32[2,128]{1,0:T(2,128)S(1)}, f32[2,128]{1,0:T(2,128)S(1)}, u32[]{:S(2)}, u32[]{:S(2)}) collective-permute-start(f32[2,128]{1,0:T(2,128)S(1)} %get-tuple-element.86.refs_0_), channel_id=1, source_target_pairs={{0,1},{1,0},{2,3},{3,2},{4,5},{5,4},{6,7},{7,6},{8,9},{9,8},{10,11... | collective-permute-start | bytes 3080 | tf_op jit(solution)/shard_map/ppermute | solution.py:547
  36.9 1.1 %collective-permute-done.13.refs_3_ = f32[2,128]{1,0:T(2,128)S(1)} collective-permute-done((f32[2,128]{1,0:T(2,128)S(1)}, f32[2,128]{1,0:T(2,128)S(1)}, u32[]{:S(2)}, u32[]{:S(2)}) %collective-permute-start.13) | collective-permute-done | bytes 1056 | tf_op jit(solution)/shard_map/ppermute | solution.py:547
  38.0 1.1 %collective-permute-done.12.refs_2_ = f32[2,128]{1,0:T(2,128)S(1)} collective-permute-done((f32[2,128]{1,0:T(2,128)S(1)}, f32[2,128]{1,0:T(2,128)S(1)}, u32[]{:S(2)}, u32[]{:S(2)}) %collective-permute-start.12) | collective-permute-done | bytes 1056 | tf_op jit(solution)/shard_map/ppermute | solution.py:547
  39.1 0.0 collective-permute-done.11.refs_1_
  39.1 1.3 %iterate.4 = (f32[8,128,128]{2,1,0:T(8,128)S(1)}, f32[8,128,128]{2,1,0:T(8,128)S(1)}, f32[2,128]{1,0:T(2,128)S(1)}) custom-call(s32[8,88]{1,0:T(8,128)S(4)} %get-tuple-element.60.plan, bf16[2,81,128,128]{3,2,1,0:T(8,128)(2,1)S(1)} %get-tuple-element.80.buf, f32[8,128,128]{2,1,0:T(8,128)S(1)} %get-tuple-element.84.vec_in, ...), custom_call_target="tpu_custom_call" | custom-call | flops 671088640 | bytes 5242880 | tf_op jit(solution)/shard_map/iterate/pallas_call | solution.py:711
  40.5 0.4 collective-permute-start.16
  40.8 0.4 collective-permute-start.15
  41.2 1.2 %collective-permute-start.14 = (f32[2,128]{1,0:T(2,128)S(1)}, f32[2,128]{1,0:T(2,128)S(1)}, u32[]{:S(2)}, u32[]{:S(2)}) collective-permute-start(f32[2,128]{1,0:T(2,128)S(1)} %get-tuple-element.89.refs_0_), channel_id=1, source_target_pairs={{0,1},{1,0},{2,3},{3,2},{4,5},{5,4},{6,7},{7,6},{8,9},{9,8},{10,11... | collective-permute-start | bytes 3080 | tf_op jit(solution)/shard_map/ppermute | solution.py:547
  42.4 1.1 %collective-permute-done.16.refs_3_ = f32[2,128]{1,0:T(2,128)S(1)} collective-permute-done((f32[2,128]{1,0:T(2,128)S(1)}, f32[2,128]{1,0:T(2,128)S(1)}, u32[]{:S(2)}, u32[]{:S(2)}) %collective-permute-start.16) | collective-permute-done | bytes 1056 | tf_op jit(solution)/shard_map/ppermute | solution.py:547
  43.5 0.9 %collective-permute-done.15.refs_2_ = f32[2,128]{1,0:T(2,128)S(1)} collective-permute-done((f32[2,128]{1,0:T(2,128)S(1)}, f32[2,128]{1,0:T(2,128)S(1)}, u32[]{:S(2)}, u32[]{:S(2)}) %collective-permute-start.15) | collective-permute-done | bytes 1056 | tf_op jit(solution)/shard_map/ppermute | solution.py:547
  44.4 0.0 collective-permute-done.14.refs_1_
  44.4 1.3 %iterate.5 = (f32[8,128,128]{2,1,0:T(8,128)S(1)}, f32[8,128,128]{2,1,0:T(8,128)S(1)}, f32[2,128]{1,0:T(2,128)S(1)}) custom-call(s32[8,88]{1,0:T(8,128)S(4)} %get-tuple-element.60.plan, bf16[2,81,128,128]{3,2,1,0:T(8,128)(2,1)S(1)} %get-tuple-element.80.buf, f32[8,128,128]{2,1,0:T(8,128)S(1)} %get-tuple-element.87.vec_in, ...), custom_call_target="tpu_custom_call" | custom-call | flops 671088640 | bytes 5242880 | tf_op jit(solution)/shard_map/iterate/pallas_call | solution.py:711
  45.7 0.4 collective-permute-start.19
  46.1 0.6 %collective-permute-start.18 = (f32[2,128]{1,0:T(2,128)S(1)}, f32[2,128]{1,0:T(2,128)S(1)}, u32[]{:S(2)}, u32[]{:S(2)}) collective-permute-start(f32[2,128]{1,0:T(2,128)S(1)} %get-tuple-element.92.refs_0_), channel_id=1, source_target_pairs={{0,2},{1,3},{2,0},{3,1},{4,6},{5,7},{6,4},{7,5},{8,10},{9,11},{10,... | collective-permute-start | bytes 3080 | tf_op jit(solution)/shard_map/ppermute | solution.py:547
  46.7 1.0 %collective-permute-start.17 = (f32[2,128]{1,0:T(2,128)S(1)}, f32[2,128]{1,0:T(2,128)S(1)}, u32[]{:S(2)}, u32[]{:S(2)}) collective-permute-start(f32[2,128]{1,0:T(2,128)S(1)} %get-tuple-element.92.refs_0_), channel_id=1, source_target_pairs={{0,1},{1,0},{2,3},{3,2},{4,5},{5,4},{6,7},{7,6},{8,9},{9,8},{10,11... | collective-permute-start | bytes 3080 | tf_op jit(solution)/shard_map/ppermute | solution.py:547
  47.6 1.1 %collective-permute-done.19.refs_3_ = f32[2,128]{1,0:T(2,128)S(1)} collective-permute-done((f32[2,128]{1,0:T(2,128)S(1)}, f32[2,128]{1,0:T(2,128)S(1)}, u32[]{:S(2)}, u32[]{:S(2)}) %collective-permute-start.19) | collective-permute-done | bytes 1056 | tf_op jit(solution)/shard_map/ppermute | solution.py:547
  48.8 0.9 %collective-permute-done.18.refs_2_ = f32[2,128]{1,0:T(2,128)S(1)} collective-permute-done((f32[2,128]{1,0:T(2,128)S(1)}, f32[2,128]{1,0:T(2,128)S(1)}, u32[]{:S(2)}, u32[]{:S(2)}) %collective-permute-start.18) | collective-permute-done | bytes 1056 | tf_op jit(solution)/shard_map/ppermute | solution.py:547
  49.7 0.0 collective-permute-done.17.refs_1_
  49.7 0.4 last.1
  50.0 0.0 copy-start.2
  50.0 0.4 collective-permute-start.22
  50.4 0.5 collective-permute-start.21
  51.0 1.0 %collective-permute-start.20 = (f32[2,128]{1,0:T(2,128)S(1)}, f32[2,128]{1,0:T(2,128)S(1)}, u32[]{:S(2)}, u32[]{:S(2)}) collective-permute-start(f32[2,128]{1,0:T(2,128)S(1)} %get-tuple-element.94.refs_0_), channel_id=1, source_target_pairs={{0,1},{1,0},{2,3},{3,2},{4,5},{5,4},{6,7},{7,6},{8,9},{9,8},{10,11... | collective-permute-start | bytes 3080 | tf_op jit(solution)/shard_map/ppermute | solution.py:547
  52.0 0.2 turn.1.vec
  52.2 0.9 %collective-permute-done.22.refs_3_ = f32[2,128]{1,0:T(2,128)S(1)} collective-permute-done((f32[2,128]{1,0:T(2,128)S(1)}, f32[2,128]{1,0:T(2,128)S(1)}, u32[]{:S(2)}, u32[]{:S(2)}) %collective-permute-start.22) | collective-permute-done | bytes 1056 | tf_op jit(solution)/shard_map/ppermute | solution.py:547
  53.1 0.9 %collective-permute-done.21.refs_2_ = f32[2,128]{1,0:T(2,128)S(1)} collective-permute-done((f32[2,128]{1,0:T(2,128)S(1)}, f32[2,128]{1,0:T(2,128)S(1)}, u32[]{:S(2)}, u32[]{:S(2)}) %collective-permute-start.21) | collective-permute-done | bytes 1056 | tf_op jit(solution)/shard_map/ppermute | solution.py:547
  54.0 0.0 collective-permute-done.20.refs_1_
  54.0 0.9 %psi.1 = bf16[8,128,128]{2,1,0:T(8,128)(2,1)} custom-call(s32[8,88]{1,0:T(8,128)S(4)} %get-tuple-element.60.plan, f32[8,128,128]{2,1,0:T(8,128)S(1)} %turn.1.vec, f32[2,128]{1,0:T(2,128)S(1)} %get-tuple-element.94.refs_0_, f32[2,128]{1,0:T(2,128)S(1)} %collective-permute-done.20.refs_1_, f32[2,128]{1,0:T(2,128)S(1)} %collective-permute-done.21.refs_2_, ...), custom_call_target="tpu_custom_call" | custom-call | bytes 524288 | tf_op jit(solution)/shard_map/psi/pallas_call | solution.py:742
  54.9 0.0 copy-done.2
  (4 shorter events, 0.0 us)
Async XLA Ops:
  0.6 12.0 %collective-permute-start.2 = (bf16[8,128,128]{2,1,0:T(8,128)(2,1)}, bf16[8,128,128]{2,1,0:T(8,128)(2,1)}, u32[]{:S(2)}, u32[]{:S(2)}) collective-permute-start(bf16[8,128,128]{2,1,0:T(8,128)(2,1)} %bitcast.8), channel_id=1, source_target_pairs={{0,4},{4,0},{8,12},{12,8},{1,5},{5,1},{9,13},{13,9},{2,6},{6,2},{1... | collective-permute-start | bytes 786440 | tf_op jit(solution)/shard_map/ppermute | solution.py:547
  3.7 8.9 %collective-permute-start.4 = (f32[8,128]{1,0:T(8,128)}, f32[8,128]{1,0:T(8,128)S(1)}, u32[]{:S(2)}, u32[]{:S(2)}) collective-permute-start(f32[8,128]{1,0:T(8,128)} %bitcast.10), channel_id=1, source_target_pairs={{0,12},{4,8},{8,4},{12,0},{1,13},{5,9},{9,5},{13,1},{2,14},{6,10},... | collective-permute-start | bytes 12296 | tf_op jit(solution)/shard_map/ppermute | solution.py:547
  6.2 6.5 %collective-permute-start.3 = (f32[8,128]{1,0:T(8,128)}, f32[8,128]{1,0:T(8,128)S(1)}, u32[]{:S(2)}, u32[]{:S(2)}) collective-permute-start(f32[8,128]{1,0:T(8,128)} %bitcast.11), channel_id=1, source_target_pairs={{0,8},{4,12},{8,0},{12,4},{1,9},{5,13},{9,1},{13,5},{2,10},{6,14},... | collective-permute-start | bytes 12296 | tf_op jit(solution)/shard_map/ppermute | solution.py:547
  8.9 3.8 %copy-start.3 = (bf16[1568,128]{1,0:T(8,128)(2,1)}, bf16[1568,128]{1,0:T(8,128)(2,1)S(1)}, u32[]{:S(2)}) copy-start(bf16[1568,128]{1,0:T(8,128)(2,1)S(1)} %get-tuple-element.72.refs_1_) | copy-start | bytes 1204228
  8.9 12.5 %collective-permute-start.5 = (bf16[1600,128]{1,0:T(8,128)(2,1)S(1)}, bf16[1600,128]{1,0:T(8,128)(2,1)S(1)}, u32[]{:S(2)}, u32[]{:S(2)}) collective-permute-start(bf16[1600,128]{1,0:T(8,128)(2,1)S(1)} %get-tuple-element.62), channel_id=1, source_target_pairs={{0,4},{4,0},{8,12},{12,8},{1,5},{5,1},{9,13},{13,9},{2,6},{6,2},{1... | collective-permute-start | bytes 1228808 | tf_op jit(solution)/shard_map/ppermute | solution.py:547
  12.7 0.6 %copy-start.4 = (f32[8,128]{1,0:T(8,128)}, f32[8,128]{1,0:T(8,128)S(1)}, u32[]{:S(2)}) copy-start(f32[8,128]{1,0:T(8,128)S(1)} %collective-permute-done.4.refs_2_.refs_4_) | copy-start | bytes 12292
  12.7 0.6 %copy-start.5 = (f32[8,128]{1,0:T(8,128)}, f32[8,128]{1,0:T(8,128)S(1)}, u32[]{:S(2)}) copy-start(f32[8,128]{1,0:T(8,128)S(1)} %collective-permute-done.3.refs_1_.refs_3_) | copy-start | bytes 12292
  13.3 2.4 %copy-start = (bf16[1,8,128,128]{3,2,1,0:T(8,128)(2,1)S(1)}, bf16[1,8,128,128]{3,2,1,0:T(8,128)(2,1)}, u32[]{:S(2)}) copy-start(bf16[1,8,128,128]{3,2,1,0:T(8,128)(2,1)} %param.10) | copy-start | bytes 786436
  13.3 2.4 %copy-start.1 = (f32[1,8,128]{2,1,0:T(8,128)S(1)}, f32[1,8,128]{2,1,0:T(8,128)}, u32[]{:S(2)}) copy-start(f32[1,8,128]{2,1,0:T(8,128)} %param.11) | copy-start | bytes 12292
  13.6 13.3 %collective-permute-start.7 = (bf16[1040,128]{1,0:T(8,128)(2,1)S(1)}, bf16[1040,128]{1,0:T(8,128)(2,1)S(1)}, u32[]{:S(2)}, u32[]{:S(2)}) collective-permute-start(bf16[1040,128]{1,0:T(8,128)(2,1)S(1)} %get-tuple-element.74), channel_id=1, source_target_pairs={{0,4},{4,0},{8,12},{12,8},{1,5},{5,1},{9,13},{13,9},{2,6},{6,2},{1... | collective-permute-start | bytes 798728 | tf_op jit(solution)/shard_map/ppermute | solution.py:547
  14.1 14.2 %collective-permute-start.6 = (bf16[528,128]{1,0:T(8,128)(2,1)S(1)}, bf16[528,128]{1,0:T(8,128)(2,1)S(1)}, u32[]{:S(2)}, u32[]{:S(2)}) collective-permute-start(bf16[528,128]{1,0:T(8,128)(2,1)S(1)} %get-tuple-element.73), channel_id=1, source_target_pairs={{0,4},{4,0},{8,12},{12,8},{1,5},{5,1},{9,13},{13,9},{2,6},{6,2},{1... | collective-permute-start | bytes 405512 | tf_op jit(solution)/shard_map/ppermute | solution.py:547
  29.9 3.1 %collective-permute-start.10 = (f32[2,128]{1,0:T(2,128)S(1)}, f32[2,128]{1,0:T(2,128)S(1)}, u32[]{:S(2)}, u32[]{:S(2)}) collective-permute-start(f32[2,128]{1,0:T(2,128)S(1)} %get-tuple-element.83.refs_0_), channel_id=1, source_target_pairs={{0,3},{1,2},{2,1},{3,0},{4,7},{5,6},{6,5},{7,4},{8,11},{9,10},{10,... | collective-permute-start | bytes 3080 | tf_op jit(solution)/shard_map/ppermute | solution.py:547
  30.0 3.6 %collective-permute-start.9 = (f32[2,128]{1,0:T(2,128)S(1)}, f32[2,128]{1,0:T(2,128)S(1)}, u32[]{:S(2)}, u32[]{:S(2)}) collective-permute-start(f32[2,128]{1,0:T(2,128)S(1)} %get-tuple-element.83.refs_0_), channel_id=1, source_target_pairs={{0,2},{1,3},{2,0},{3,1},{4,6},{5,7},{6,4},{7,5},{8,10},{9,11},{10,... | collective-permute-start | bytes 3080 | tf_op jit(solution)/shard_map/ppermute | solution.py:547
  30.3 3.3 %collective-permute-start.8 = (f32[2,128]{1,0:T(2,128)S(1)}, f32[2,128]{1,0:T(2,128)S(1)}, u32[]{:S(2)}, u32[]{:S(2)}) collective-permute-start(f32[2,128]{1,0:T(2,128)S(1)} %get-tuple-element.83.refs_0_), channel_id=1, source_target_pairs={{0,1},{1,0},{2,3},{3,2},{4,5},{5,4},{6,7},{7,6},{8,9},{9,8},{10,11... | collective-permute-start | bytes 3080 | tf_op jit(solution)/shard_map/ppermute | solution.py:547
  34.9 3.1 %collective-permute-start.13 = (f32[2,128]{1,0:T(2,128)S(1)}, f32[2,128]{1,0:T(2,128)S(1)}, u32[]{:S(2)}, u32[]{:S(2)}) collective-permute-start(f32[2,128]{1,0:T(2,128)S(1)} %get-tuple-element.86.refs_0_), channel_id=1, source_target_pairs={{0,3},{1,2},{2,1},{3,0},{4,7},{5,6},{6,5},{7,4},{8,11},{9,10},{10,... | collective-permute-start | bytes 3080 | tf_op jit(solution)/shard_map/ppermute | solution.py:547
  35.5 3.6 %collective-permute-start.12 = (f32[2,128]{1,0:T(2,128)S(1)}, f32[2,128]{1,0:T(2,128)S(1)}, u32[]{:S(2)}, u32[]{:S(2)}) collective-permute-start(f32[2,128]{1,0:T(2,128)S(1)} %get-tuple-element.86.refs_0_), channel_id=1, source_target_pairs={{0,2},{1,3},{2,0},{3,1},{4,6},{5,7},{6,4},{7,5},{8,10},{9,11},{10,... | collective-permute-start | bytes 3080 | tf_op jit(solution)/shard_map/ppermute | solution.py:547
  36.1 3.0 %collective-permute-start.11 = (f32[2,128]{1,0:T(2,128)S(1)}, f32[2,128]{1,0:T(2,128)S(1)}, u32[]{:S(2)}, u32[]{:S(2)}) collective-permute-start(f32[2,128]{1,0:T(2,128)S(1)} %get-tuple-element.86.refs_0_), channel_id=1, source_target_pairs={{0,1},{1,0},{2,3},{3,2},{4,5},{5,4},{6,7},{7,6},{8,9},{9,8},{10,11... | collective-permute-start | bytes 3080 | tf_op jit(solution)/shard_map/ppermute | solution.py:547
  40.5 3.1 %collective-permute-start.16 = (f32[2,128]{1,0:T(2,128)S(1)}, f32[2,128]{1,0:T(2,128)S(1)}, u32[]{:S(2)}, u32[]{:S(2)}) collective-permute-start(f32[2,128]{1,0:T(2,128)S(1)} %get-tuple-element.89.refs_0_), channel_id=1, source_target_pairs={{0,3},{1,2},{2,1},{3,0},{4,7},{5,6},{6,5},{7,4},{8,11},{9,10},{10,... | collective-permute-start | bytes 3080 | tf_op jit(solution)/shard_map/ppermute | solution.py:547
  40.8 3.6 %collective-permute-start.15 = (f32[2,128]{1,0:T(2,128)S(1)}, f32[2,128]{1,0:T(2,128)S(1)}, u32[]{:S(2)}, u32[]{:S(2)}) collective-permute-start(f32[2,128]{1,0:T(2,128)S(1)} %get-tuple-element.89.refs_0_), channel_id=1, source_target_pairs={{0,2},{1,3},{2,0},{3,1},{4,6},{5,7},{6,4},{7,5},{8,10},{9,11},{10,... | collective-permute-start | bytes 3080 | tf_op jit(solution)/shard_map/ppermute | solution.py:547
  41.2 3.2 %collective-permute-start.14 = (f32[2,128]{1,0:T(2,128)S(1)}, f32[2,128]{1,0:T(2,128)S(1)}, u32[]{:S(2)}, u32[]{:S(2)}) collective-permute-start(f32[2,128]{1,0:T(2,128)S(1)} %get-tuple-element.89.refs_0_), channel_id=1, source_target_pairs={{0,1},{1,0},{2,3},{3,2},{4,5},{5,4},{6,7},{7,6},{8,9},{9,8},{10,11... | collective-permute-start | bytes 3080 | tf_op jit(solution)/shard_map/ppermute | solution.py:547
  45.7 3.1 %collective-permute-start.19 = (f32[2,128]{1,0:T(2,128)S(1)}, f32[2,128]{1,0:T(2,128)S(1)}, u32[]{:S(2)}, u32[]{:S(2)}) collective-permute-start(f32[2,128]{1,0:T(2,128)S(1)} %get-tuple-element.92.refs_0_), channel_id=1, source_target_pairs={{0,3},{1,2},{2,1},{3,0},{4,7},{5,6},{6,5},{7,4},{8,11},{9,10},{10,... | collective-permute-start | bytes 3080 | tf_op jit(solution)/shard_map/ppermute | solution.py:547
  46.1 3.6 %collective-permute-start.18 = (f32[2,128]{1,0:T(2,128)S(1)}, f32[2,128]{1,0:T(2,128)S(1)}, u32[]{:S(2)}, u32[]{:S(2)}) collective-permute-start(f32[2,128]{1,0:T(2,128)S(1)} %get-tuple-element.92.refs_0_), channel_id=1, source_target_pairs={{0,2},{1,3},{2,0},{3,1},{4,6},{5,7},{6,4},{7,5},{8,10},{9,11},{10,... | collective-permute-start | bytes 3080 | tf_op jit(solution)/shard_map/ppermute | solution.py:547
  46.7 3.0 %collective-permute-start.17 = (f32[2,128]{1,0:T(2,128)S(1)}, f32[2,128]{1,0:T(2,128)S(1)}, u32[]{:S(2)}, u32[]{:S(2)}) collective-permute-start(f32[2,128]{1,0:T(2,128)S(1)} %get-tuple-element.92.refs_0_), channel_id=1, source_target_pairs={{0,1},{1,0},{2,3},{3,2},{4,5},{5,4},{6,7},{7,6},{8,9},{9,8},{10,11... | collective-permute-start | bytes 3080 | tf_op jit(solution)/shard_map/ppermute | solution.py:547
  50.0 4.8 %copy-start.2 = (f32[1,128]{1,0:T(1,128)}, f32[1,128]{1,0:T(1,128)S(1)}, u32[]{:S(2)}) copy-start(f32[1,128]{1,0:T(1,128)S(1)} %get-tuple-element.95) | copy-start | bytes 1540
  50.0 3.1 %collective-permute-start.22 = (f32[2,128]{1,0:T(2,128)S(1)}, f32[2,128]{1,0:T(2,128)S(1)}, u32[]{:S(2)}, u32[]{:S(2)}) collective-permute-start(f32[2,128]{1,0:T(2,128)S(1)} %get-tuple-element.94.refs_0_), channel_id=1, source_target_pairs={{0,3},{1,2},{2,1},{3,0},{4,7},{5,6},{6,5},{7,4},{8,11},{9,10},{10,... | collective-permute-start | bytes 3080 | tf_op jit(solution)/shard_map/ppermute | solution.py:547
  50.4 3.6 %collective-permute-start.21 = (f32[2,128]{1,0:T(2,128)S(1)}, f32[2,128]{1,0:T(2,128)S(1)}, u32[]{:S(2)}, u32[]{:S(2)}) collective-permute-start(f32[2,128]{1,0:T(2,128)S(1)} %get-tuple-element.94.refs_0_), channel_id=1, source_target_pairs={{0,2},{1,3},{2,0},{3,1},{4,6},{5,7},{6,4},{7,5},{8,10},{9,11},{10,... | collective-permute-start | bytes 3080 | tf_op jit(solution)/shard_map/ppermute | solution.py:547
  51.0 3.0 %collective-permute-start.20 = (f32[2,128]{1,0:T(2,128)S(1)}, f32[2,128]{1,0:T(2,128)S(1)}, u32[]{:S(2)}, u32[]{:S(2)}) collective-permute-start(f32[2,128]{1,0:T(2,128)S(1)} %get-tuple-element.94.refs_0_), channel_id=1, source_target_pairs={{0,1},{1,0},{2,3},{3,2},{4,5},{5,4},{6,7},{7,6},{8,9},{9,8},{10,11... | collective-permute-start | bytes 3080 | tf_op jit(solution)/shard_map/ppermute | solution.py:547

commit v2 on v0

--- a/solution.py
+++ b/solution.py
@@ -562,7 +562,7 @@
     pairs = -(-blocks // (2 * group)) * group
     base = min(pairs, -(-pairs * 3 // 5 // (2 * group)) * 2 * group)
     third = max(base // 6 // group, 1) * group
-    marks = [0, base // 2, base - third, base, min(base + third, pairs), pairs]
+    marks = [0, base - 2 * third, base - third, base, min(base + third, pairs), pairs]
     cuts = [(a, b) for a, b in zip(marks[:-1], marks[1:]) if a < b]
     usual = 3
     tails = [-(-2 * (c[1] - c[0]) // 16) * 16 for c in cuts]

time: 54.4 us -> 54.6 us (level)
  transfers between devices with their start and end apart: 21 -> 21, of which waited for: 13 -> 14; matrix products, arithmetic and copies ran while one was open for 0% -> 0% of each run, Pallas kernels for 16% -> 16%
where the time goes in v2:
time: 54.6 us; the launch traced here: 54.4 us
  starting transfers between devices  19.3 us (35%)
  waiting for transfers between devices  18.5 us (34%)
  Pallas kernels  15 us (27%)
  between operations  0.95 us (2%)
  local copies, waits for them, and re-layouts  0.71 us (1%)
    ppermute x21, starting transfers between devices, swapped(): return lax.ppermute(value, axis, [(k, k ^ mask) for k in range(size)])  19.3 us
    ppermute x21, waiting for transfers between devices, swapped(): return lax.ppermute(value, axis, [(k, k ^ mask) for k in range(size)])  18.5 us
    pallas_call x3, Pallas kernels, local(): pl.pallas_call(functools.partial(iter_kernel, count, tensor), out_shape=[...  3.97 us
    pallas_call x1, Pallas kernels, local(): pl.pallas_call(functools.partial(own_kernel, group, chans), out_shape=[bu...  3.18 us
    pallas_call x1, Pallas kernels, local(): pl.pallas_call(functools.partial(pack_kernel, cuts[0], cuts[usual:], grou...  2.71 us
    pallas_call x1, Pallas kernels, local(): pl.pallas_call(functools.partial(mid_kernel, cuts[1], group), out_shape=[...  1.32 us
  transfers between devices with their start and end apart: 21, of which 14 were waited for; matrix products, arithmetic and copies ran while one was open for 0% of the time, Pallas kernels for 16%

profile of v2, /device:TPU:0, one launch (start us, length us, event | category | flops | bytes accessed | tf_op | source)
XLA Modules:
  0.0 54.4 jit_solution(12693003211160939052)
XLA Ops:
  0.6 3.1 %collective-permute-start.2 = (bf16[8,128,128]{2,1,0:T(8,128)(2,1)}, bf16[8,128,128]{2,1,0:T(8,128)(2,1)S(1)}, u32[]{:S(2)}, u32[]{:S(2)}) collective-permute-start(bf16[8,128,128]{2,1,0:T(8,128)(2,1)} %bitcast.8), channel_id=1, source_target_pairs={{0,4},{4,0},{8,12},{12,8},{1,5},{5,1},{9,13},{13,9},{2,6},{6,2},{1... | collective-permute-start | bytes 786440 | tf_op jit(solution)/shard_map/ppermute | solution.py:545
  3.7 2.5 %collective-permute-start.4 = (f32[8,128]{1,0:T(8,128)}, f32[8,128]{1,0:T(8,128)S(1)}, u32[]{:S(2)}, u32[]{:S(2)}) collective-permute-start(f32[8,128]{1,0:T(8,128)} %bitcast.10), channel_id=1, source_target_pairs={{0,12},{4,8},{8,4},{12,0},{1,13},{5,9},{9,5},{13,1},{2,14},{6,10},... | collective-permute-start | bytes 12296 | tf_op jit(solution)/shard_map/ppermute | solution.py:545
  6.2 0.1 collective-permute-start.3
  6.3 2.7 %pack.1 = (bf16[528,128]{1,0:T(8,128)(2,1)}, bf16[1568,128]{1,0:T(8,128)(2,1)}, bf16[2112,128]{1,0:T(8,128)(2,1)S(1)}, s32[8,88]{1,0:T(8,128)S(4)}, s32[1]{0:T(128)S(4)}, /*index=5*/bf16[80,128,128]{2,1,0:T(8,128)(2,1)S(1)}) custom-call(s32[8,10]{1,0:T(8,128)} %mask_hbm.1, s32[8]{0:T(128)} %ranks_hbm.1, f32[8,128]{1,0:T(8,128)} %bitcast.12, ...), custom_call_target="tpu_custom_call" | custom-call | flops 10000000 | bytes 5242880 | tf_op jit(solution)/shard_map/pack/pallas_call | solution.py:586
  9.1 1.9 %collective-permute-start.5 = (bf16[2112,128]{1,0:T(8,128)(2,1)S(1)}, bf16[2112,128]{1,0:T(8,128)(2,1)S(1)}, u32[]{:S(2)}, u32[]{:S(2)}) collective-permute-start(bf16[2112,128]{1,0:T(8,128)(2,1)S(1)} %get-tuple-element.62), channel_id=1, source_target_pairs={{0,4},{4,0},{8,12},{12,8},{1,5},{5,1},{9,13},{13,9},{2,6},{6,2},{1... | collective-permute-start | bytes 1622024 | tf_op jit(solution)/shard_map/ppermute | solution.py:545
  10.9 1.7 %collective-permute-done.4.refs_2_.refs_4_ = f32[8,128]{1,0:T(8,128)S(1)} collective-permute-done((f32[8,128]{1,0:T(8,128)}, f32[8,128]{1,0:T(8,128)S(1)}, u32[]{:S(2)}, u32[]{:S(2)}) %collective-permute-start.4) | collective-permute-done | bytes 4128 | tf_op jit(solution)/shard_map/ppermute | solution.py:545
  12.7 0.0 collective-permute-done.3.refs_1_.refs_3_
  12.7 0.0 copy-start.5
  12.7 0.0 collective-permute-done.2.other_site.refs_2_
  12.7 0.0 copy-start.3
  12.7 0.6 %copy-done.4 = f32[8,128]{1,0:T(8,128)} copy-done((f32[8,128]{1,0:T(8,128)}, f32[8,128]{1,0:T(8,128)S(1)}, u32[]{:S(2)}) %copy-start.4) | copy-done | bytes 4120
  13.3 0.0 copy-done.5
  13.3 0.1 copy-done.3
  13.4 0.2 rest.1
  13.6 0.6 %collective-permute-start.7 = (bf16[528,128]{1,0:T(8,128)(2,1)S(1)}, bf16[528,128]{1,0:T(8,128)(2,1)S(1)}, u32[]{:S(2)}, u32[]{:S(2)}) collective-permute-start(bf16[528,128]{1,0:T(8,128)(2,1)S(1)} %get-tuple-element.74), channel_id=1, source_target_pairs={{0,4},{4,0},{8,12},{12,8},{1,5},{5,1},{9,13},{13,9},{2,6},{6,2},{1... | collective-permute-start | bytes 405512 | tf_op jit(solution)/shard_map/ppermute | solution.py:545
  14.2 1.5 %collective-permute-start.6 = (bf16[528,128]{1,0:T(8,128)(2,1)S(1)}, bf16[528,128]{1,0:T(8,128)(2,1)S(1)}, u32[]{:S(2)}, u32[]{:S(2)}) collective-permute-start(bf16[528,128]{1,0:T(8,128)(2,1)S(1)} %get-tuple-element.73), channel_id=1, source_target_pairs={{0,4},{4,0},{8,12},{12,8},{1,5},{5,1},{9,13},{13,9},{2,6},{6,2},{1... | collective-permute-start | bytes 405512 | tf_op jit(solution)/shard_map/ppermute | solution.py:545
  15.7 0.0 copy-done
  15.7 0.0 copy-done.1
  15.7 3.2 %own.1 = (bf16[2,81,128,128]{3,2,1,0:T(8,128)(2,1)S(1)}, f32[2,8,16,128]{3,2,1,0:T(8,128)S(1)}, f32[8,128]{1,0:T(8,128)S(1)}, f32[8,128,128]{2,1,0:T(8,128)S(1)}, s32[8,88]{1,0:T(8,128)S(4)}) custom-call(s32[8,88]{1,0:T(8,128)S(4)} %get-tuple-element.58.table, bf16[80,128,128]{2,1,0:T(8,128)(2,1)S(1)} %get-tuple-element.59.env, ...), custom_call_target="tpu_custom_call" | custom-call | tf_op jit(solution)/shard_map/own/pallas_call | solution.py:644
  18.9 5.5 %collective-permute-done.5.chunk = bf16[2112,128]{1,0:T(8,128)(2,1)S(1)} collective-permute-done((bf16[2112,128]{1,0:T(8,128)(2,1)S(1)}, bf16[2112,128]{1,0:T(8,128)(2,1)S(1)}, u32[]{:S(2)}, u32[]{:S(2)}) %collective-permute-start.5) | collective-permute-done | bytes 540704 | tf_op jit(solution)/shard_map/ppermute | solution.py:545
  24.3 0.9 %outer.1 = (bf16[2,81,128,128]{3,2,1,0:T(8,128)(2,1)S(1)}, f32[2,8,16,128]{3,2,1,0:T(8,128)S(1)}, f32[8,128,128]{2,1,0:T(8,128)S(1)}, f32[8,128]{1,0:T(8,128)S(1)}) custom-call(s32[8,88]{1,0:T(8,128)S(4)} %get-tuple-element.60.plan, f32[8,128]{1,0:T(8,128)S(1)} %get-tuple-element.61.prefix, ...), custom_call_target="tpu_custom_call", output_to_operand_aliasing={{0}: (3, {}), {1}: (4, {})} | custom-call | tf_op jit(solution)/shard_map/outer/pallas_call | solution.py:656
  25.2 1.8 %collective-permute-done.7.chunk = bf16[528,128]{1,0:T(8,128)(2,1)S(1)} collective-permute-done((bf16[528,128]{1,0:T(8,128)(2,1)S(1)}, bf16[528,128]{1,0:T(8,128)(2,1)S(1)}, u32[]{:S(2)}, u32[]{:S(2)}) %collective-permute-start.7) | collective-permute-done | bytes 135200 | tf_op jit(solution)/shard_map/ppermute | solution.py:545
  27.0 1.3 %mid.1 = (bf16[2,81,128,128]{3,2,1,0:T(8,128)(2,1)S(1)}, f32[2,8,16,128]{3,2,1,0:T(8,128)S(1)}, f32[8,128,128]{2,1,0:T(8,128)S(1)}) custom-call(s32[8,88]{1,0:T(8,128)S(4)} %get-tuple-element.60.plan, f32[8,128,128]{2,1,0:T(8,128)S(1)} %get-tuple-element.65.outer, ...), custom_call_target="tpu_custom_call", output_to_operand_aliasing={{0}: (5, {}), {1}: (6, {})} | custom-call | tf_op jit(solution)/shard_map/mid/pallas_call | solution.py:668
  28.3 0.1 collective-permute-done.6.chunk
  28.5 1.0 %first.1 = (bf16[2,81,128,128]{3,2,1,0:T(8,128)(2,1)S(1)}, f32[2,8,16,128]{3,2,1,0:T(8,128)S(1)}, f32[8,128,128]{2,1,0:T(8,128)S(1)}, f32[2,128]{1,0:T(2,128)S(1)}) custom-call(s32[8,88]{1,0:T(8,128)S(4)} %get-tuple-element.60.plan, f32[8,128,128]{2,1,0:T(8,128)S(1)} %get-tuple-element.65.outer, ...), custom_call_target="tpu_custom_call", output_to_operand_aliasing={{0}: (7, {}), {1}: (8, {}), {2}: (9, {})} | custom-call | flops 671088640 | bytes 5242880 | tf_op jit(solution)/shard_map/first/pallas_call | solution.py:681
  29.5 0.1 collective-permute-start.10
  29.6 0.9 %collective-permute-start.9 = (f32[2,128]{1,0:T(2,128)S(1)}, f32[2,128]{1,0:T(2,128)S(1)}, u32[]{:S(2)}, u32[]{:S(2)}) collective-permute-start(f32[2,128]{1,0:T(2,128)S(1)} %get-tuple-element.83.refs_0_), channel_id=1, source_target_pairs={{0,2},{1,3},{2,0},{3,1},{4,6},{5,7},{6,4},{7,5},{8,10},{9,11},{10,... | collective-permute-start | bytes 3080 | tf_op jit(solution)/shard_map/ppermute | solution.py:545
  30.4 1.0 %collective-permute-start.8 = (f32[2,128]{1,0:T(2,128)S(1)}, f32[2,128]{1,0:T(2,128)S(1)}, u32[]{:S(2)}, u32[]{:S(2)}) collective-permute-start(f32[2,128]{1,0:T(2,128)S(1)} %get-tuple-element.83.refs_0_), channel_id=1, source_target_pairs={{0,1},{1,0},{2,3},{3,2},{4,5},{5,4},{6,7},{7,6},{8,9},{9,8},{10,11... | collective-permute-start | bytes 3080 | tf_op jit(solution)/shard_map/ppermute | solution.py:545
  31.4 0.3 diagonal.1.dh
  31.7 0.9 %collective-permute-done.10.refs_3_ = f32[2,128]{1,0:T(2,128)S(1)} collective-permute-done((f32[2,128]{1,0:T(2,128)S(1)}, f32[2,128]{1,0:T(2,128)S(1)}, u32[]{:S(2)}, u32[]{:S(2)}) %collective-permute-start.10) | collective-permute-done | bytes 1056 | tf_op jit(solution)/shard_map/ppermute | solution.py:545
  32.6 0.7 %collective-permute-done.9.refs_2_ = f32[2,128]{1,0:T(2,128)S(1)} collective-permute-done((f32[2,128]{1,0:T(2,128)S(1)}, f32[2,128]{1,0:T(2,128)S(1)}, u32[]{:S(2)}, u32[]{:S(2)}) %collective-permute-start.9) | collective-permute-done | bytes 1056 | tf_op jit(solution)/shard_map/ppermute | solution.py:545
  33.2 0.0 collective-permute-done.8.refs_1_
  33.2 1.3 %iterate.3 = (f32[8,128,128]{2,1,0:T(8,128)S(1)}, f32[8,128,128]{2,1,0:T(8,128)S(1)}, f32[2,128]{1,0:T(2,128)S(1)}) custom-call(s32[8,88]{1,0:T(8,128)S(4)} %get-tuple-element.60.plan, bf16[2,81,128,128]{3,2,1,0:T(8,128)(2,1)S(1)} %get-tuple-element.80.buf, f32[8,128,128]{2,1,0:T(8,128)S(1)} %get-tuple-element.67.vec.vec_in, ...), custom_call_target="tpu_custom_call" | custom-call | flops 671088640 | bytes 5242880 | tf_op jit(solution)/shard_map/iterate/pallas_call | solution.py:709
  34.5 0.6 %collective-permute-start.13 = (f32[2,128]{1,0:T(2,128)S(1)}, f32[2,128]{1,0:T(2,128)S(1)}, u32[]{:S(2)}, u32[]{:S(2)}) collective-permute-start(f32[2,128]{1,0:T(2,128)S(1)} %get-tuple-element.86.refs_0_), channel_id=1, source_target_pairs={{0,3},{1,2},{2,1},{3,0},{4,7},{5,6},{6,5},{7,4},{8,11},{9,10},{10,... | collective-permute-start | bytes 3080 | tf_op jit(solution)/shard_map/ppermute | solution.py:545
  35.1 0.8 %collective-permute-start.12 = (f32[2,128]{1,0:T(2,128)S(1)}, f32[2,128]{1,0:T(2,128)S(1)}, u32[]{:S(2)}, u32[]{:S(2)}) collective-permute-start(f32[2,128]{1,0:T(2,128)S(1)} %get-tuple-element.86.refs_0_), channel_id=1, source_target_pairs={{0,2},{1,3},{2,0},{3,1},{4,6},{5,7},{6,4},{7,5},{8,10},{9,11},{10,... | collective-permute-start | bytes 3080 | tf_op jit(solution)/shard_map/ppermute | solution.py:545
  35.9 0.5 collective-permute-start.11
  36.5 1.1 %collective-permute-done.13.refs_3_ = f32[2,128]{1,0:T(2,128)S(1)} collective-permute-done((f32[2,128]{1,0:T(2,128)S(1)}, f32[2,128]{1,0:T(2,128)S(1)}, u32[]{:S(2)}, u32[]{:S(2)}) %collective-permute-start.13) | collective-permute-done | bytes 1056 | tf_op jit(solution)/shard_map/ppermute | solution.py:545
  37.6 1.1 %collective-permute-done.12.refs_2_ = f32[2,128]{1,0:T(2,128)S(1)} collective-permute-done((f32[2,128]{1,0:T(2,128)S(1)}, f32[2,128]{1,0:T(2,128)S(1)}, u32[]{:S(2)}, u32[]{:S(2)}) %collective-permute-start.12) | collective-permute-done | bytes 1056 | tf_op jit(solution)/shard_map/ppermute | solution.py:545
  38.7 0.0 collective-permute-done.11.refs_1_
  38.7 1.3 %iterate.4 = (f32[8,128,128]{2,1,0:T(8,128)S(1)}, f32[8,128,128]{2,1,0:T(8,128)S(1)}, f32[2,128]{1,0:T(2,128)S(1)}) custom-call(s32[8,88]{1,0:T(8,128)S(4)} %get-tuple-element.60.plan, bf16[2,81,128,128]{3,2,1,0:T(8,128)(2,1)S(1)} %get-tuple-element.80.buf, f32[8,128,128]{2,1,0:T(8,128)S(1)} %get-tuple-element.84.vec_in, ...), custom_call_target="tpu_custom_call" | custom-call | flops 671088640 | bytes 5242880 | tf_op jit(solution)/shard_map/iterate/pallas_call | solution.py:709
  40.1 0.1 collective-permute-start.16
  40.2 0.8 %collective-permute-start.15 = (f32[2,128]{1,0:T(2,128)S(1)}, f32[2,128]{1,0:T(2,128)S(1)}, u32[]{:S(2)}, u32[]{:S(2)}) collective-permute-start(f32[2,128]{1,0:T(2,128)S(1)} %get-tuple-element.89.refs_0_), channel_id=1, source_target_pairs={{0,2},{1,3},{2,0},{3,1},{4,6},{5,7},{6,4},{7,5},{8,10},{9,11},{10,... | collective-permute-start | bytes 3080 | tf_op jit(solution)/shard_map/ppermute | solution.py:545
  41.0 1.0 %collective-permute-start.14 = (f32[2,128]{1,0:T(2,128)S(1)}, f32[2,128]{1,0:T(2,128)S(1)}, u32[]{:S(2)}, u32[]{:S(2)}) collective-permute-start(f32[2,128]{1,0:T(2,128)S(1)} %get-tuple-element.89.refs_0_), channel_id=1, source_target_pairs={{0,1},{1,0},{2,3},{3,2},{4,5},{5,4},{6,7},{7,6},{8,9},{9,8},{10,11... | collective-permute-start | bytes 3080 | tf_op jit(solution)/shard_map/ppermute | solution.py:545
  42.0 1.1 %collective-permute-done.16.refs_3_ = f32[2,128]{1,0:T(2,128)S(1)} collective-permute-done((f32[2,128]{1,0:T(2,128)S(1)}, f32[2,128]{1,0:T(2,128)S(1)}, u32[]{:S(2)}, u32[]{:S(2)}) %collective-permute-start.16) | collective-permute-done | bytes 1056 | tf_op jit(solution)/shard_map/ppermute | solution.py:545
  43.1 0.7 %collective-permute-done.15.refs_2_ = f32[2,128]{1,0:T(2,128)S(1)} collective-permute-done((f32[2,128]{1,0:T(2,128)S(1)}, f32[2,128]{1,0:T(2,128)S(1)}, u32[]{:S(2)}, u32[]{:S(2)}) %collective-permute-start.15) | collective-permute-done | bytes 1056 | tf_op jit(solution)/shard_map/ppermute | solution.py:545
  43.8 0.0 collective-permute-done.14.refs_1_
  43.8 1.3 %iterate.5 = (f32[8,128,128]{2,1,0:T(8,128)S(1)}, f32[8,128,128]{2,1,0:T(8,128)S(1)}, f32[2,128]{1,0:T(2,128)S(1)}) custom-call(s32[8,88]{1,0:T(8,128)S(4)} %get-tuple-element.60.plan, bf16[2,81,128,128]{3,2,1,0:T(8,128)(2,1)S(1)} %get-tuple-element.80.buf, f32[8,128,128]{2,1,0:T(8,128)S(1)} %get-tuple-element.87.vec_in, ...), custom_call_target="tpu_custom_call" | custom-call | flops 671088640 | bytes 5242880 | tf_op jit(solution)/shard_map/iterate/pallas_call | solution.py:709
  45.1 0.6 %collective-permute-start.19 = (f32[2,128]{1,0:T(2,128)S(1)}, f32[2,128]{1,0:T(2,128)S(1)}, u32[]{:S(2)}, u32[]{:S(2)}) collective-permute-start(f32[2,128]{1,0:T(2,128)S(1)} %get-tuple-element.92.refs_0_), channel_id=1, source_target_pairs={{0,3},{1,2},{2,1},{3,0},{4,7},{5,6},{6,5},{7,4},{8,11},{9,10},{10,... | collective-permute-start | bytes 3080 | tf_op jit(solution)/shard_map/ppermute | solution.py:545
  45.7 0.8 %collective-permute-start.18 = (f32[2,128]{1,0:T(2,128)S(1)}, f32[2,128]{1,0:T(2,128)S(1)}, u32[]{:S(2)}, u32[]{:S(2)}) collective-permute-start(f32[2,128]{1,0:T(2,128)S(1)} %get-tuple-element.92.refs_0_), channel_id=1, source_target_pairs={{0,2},{1,3},{2,0},{3,1},{4,6},{5,7},{6,4},{7,5},{8,10},{9,11},{10,... | collective-permute-start | bytes 3080 | tf_op jit(solution)/shard_map/ppermute | solution.py:545
  46.5 0.6 %collective-permute-start.17 = (f32[2,128]{1,0:T(2,128)S(1)}, f32[2,128]{1,0:T(2,128)S(1)}, u32[]{:S(2)}, u32[]{:S(2)}) collective-permute-start(f32[2,128]{1,0:T(2,128)S(1)} %get-tuple-element.92.refs_0_), channel_id=1, source_target_pairs={{0,1},{1,0},{2,3},{3,2},{4,5},{5,4},{6,7},{7,6},{8,9},{9,8},{10,11... | collective-permute-start | bytes 3080 | tf_op jit(solution)/shard_map/ppermute | solution.py:545
  47.0 1.1 %collective-permute-done.19.refs_3_ = f32[2,128]{1,0:T(2,128)S(1)} collective-permute-done((f32[2,128]{1,0:T(2,128)S(1)}, f32[2,128]{1,0:T(2,128)S(1)}, u32[]{:S(2)}, u32[]{:S(2)}) %collective-permute-start.19) | collective-permute-done | bytes 1056 | tf_op jit(solution)/shard_map/ppermute | solution.py:545
  48.2 1.1 %collective-permute-done.18.refs_2_ = f32[2,128]{1,0:T(2,128)S(1)} collective-permute-done((f32[2,128]{1,0:T(2,128)S(1)}, f32[2,128]{1,0:T(2,128)S(1)}, u32[]{:S(2)}, u32[]{:S(2)}) %collective-permute-start.18) | collective-permute-done | bytes 1056 | tf_op jit(solution)/shard_map/ppermute | solution.py:545
  49.3 0.0 collective-permute-done.17.refs_1_
  49.3 0.4 last.1
  49.6 0.0 copy-start.2
  49.7 0.1 collective-permute-start.22
  49.8 0.8 %collective-permute-start.21 = (f32[2,128]{1,0:T(2,128)S(1)}, f32[2,128]{1,0:T(2,128)S(1)}, u32[]{:S(2)}, u32[]{:S(2)}) collective-permute-start(f32[2,128]{1,0:T(2,128)S(1)} %get-tuple-element.94.refs_0_), channel_id=1, source_target_pairs={{0,2},{1,3},{2,0},{3,1},{4,6},{5,7},{6,4},{7,5},{8,10},{9,11},{10,... | collective-permute-start | bytes 3080 | tf_op jit(solution)/shard_map/ppermute | solution.py:545
  50.6 1.0 %collective-permute-start.20 = (f32[2,128]{1,0:T(2,128)S(1)}, f32[2,128]{1,0:T(2,128)S(1)}, u32[]{:S(2)}, u32[]{:S(2)}) collective-permute-start(f32[2,128]{1,0:T(2,128)S(1)} %get-tuple-element.94.refs_0_), channel_id=1, source_target_pairs={{0,1},{1,0},{2,3},{3,2},{4,5},{5,4},{6,7},{7,6},{8,9},{9,8},{10,11... | collective-permute-start | bytes 3080 | tf_op jit(solution)/shard_map/ppermute | solution.py:545
  51.6 0.2 turn.1.vec
  51.8 0.9 %collective-permute-done.22.refs_3_ = f32[2,128]{1,0:T(2,128)S(1)} collective-permute-done((f32[2,128]{1,0:T(2,128)S(1)}, f32[2,128]{1,0:T(2,128)S(1)}, u32[]{:S(2)}, u32[]{:S(2)}) %collective-permute-start.22) | collective-permute-done | bytes 1056 | tf_op jit(solution)/shard_map/ppermute | solution.py:545
  52.7 0.7 %collective-permute-done.21.refs_2_ = f32[2,128]{1,0:T(2,128)S(1)} collective-permute-done((f32[2,128]{1,0:T(2,128)S(1)}, f32[2,128]{1,0:T(2,128)S(1)}, u32[]{:S(2)}, u32[]{:S(2)}) %collective-permute-start.21) | collective-permute-done | bytes 1056 | tf_op jit(solution)/shard_map/ppermute | solution.py:545
  53.4 0.0 collective-permute-done.20.refs_1_
  53.4 0.9 %psi.1 = bf16[8,128,128]{2,1,0:T(8,128)(2,1)} custom-call(s32[8,88]{1,0:T(8,128)S(4)} %get-tuple-element.60.plan, f32[8,128,128]{2,1,0:T(8,128)S(1)} %turn.1.vec, f32[2,128]{1,0:T(2,128)S(1)} %get-tuple-element.94.refs_0_, f32[2,128]{1,0:T(2,128)S(1)} %collective-permute-done.20.refs_1_, f32[2,128]{1,0:T(2,128)S(1)} %collective-permute-done.21.refs_2_, ...), custom_call_target="tpu_custom_call" | custom-call | bytes 524288 | tf_op jit(solution)/shard_map/psi/pallas_call | solution.py:740
  54.2 0.0 copy-done.2
  (4 shorter events, 0.0 us)
Async XLA Ops:
  0.6 12.0 %collective-permute-start.2 = (bf16[8,128,128]{2,1,0:T(8,128)(2,1)}, bf16[8,128,128]{2,1,0:T(8,128)(2,1)S(1)}, u32[]{:S(2)}, u32[]{:S(2)}) collective-permute-start(bf16[8,128,128]{2,1,0:T(8,128)(2,1)} %bitcast.8), channel_id=1, source_target_pairs={{0,4},{4,0},{8,12},{12,8},{1,5},{5,1},{9,13},{13,9},{2,6},{6,2},{1... | collective-permute-start | bytes 786440 | tf_op jit(solution)/shard_map/ppermute | solution.py:545
  3.7 8.9 %collective-permute-start.4 = (f32[8,128]{1,0:T(8,128)}, f32[8,128]{1,0:T(8,128)S(1)}, u32[]{:S(2)}, u32[]{:S(2)}) collective-permute-start(f32[8,128]{1,0:T(8,128)} %bitcast.10), channel_id=1, source_target_pairs={{0,12},{4,8},{8,4},{12,0},{1,13},{5,9},{9,5},{13,1},{2,14},{6,10},... | collective-permute-start | bytes 12296 | tf_op jit(solution)/shard_map/ppermute | solution.py:545
  6.2 6.5 %collective-permute-start.3 = (f32[8,128]{1,0:T(8,128)}, f32[8,128]{1,0:T(8,128)S(1)}, u32[]{:S(2)}, u32[]{:S(2)}) collective-permute-start(f32[8,128]{1,0:T(8,128)} %bitcast.11), channel_id=1, source_target_pairs={{0,8},{4,12},{8,0},{12,4},{1,9},{5,13},{9,1},{13,5},{2,10},{6,14},... | collective-permute-start | bytes 12296 | tf_op jit(solution)/shard_map/ppermute | solution.py:545
  9.1 15.3 %collective-permute-start.5 = (bf16[2112,128]{1,0:T(8,128)(2,1)S(1)}, bf16[2112,128]{1,0:T(8,128)(2,1)S(1)}, u32[]{:S(2)}, u32[]{:S(2)}) collective-permute-start(bf16[2112,128]{1,0:T(8,128)(2,1)S(1)} %get-tuple-element.62), channel_id=1, source_target_pairs={{0,4},{4,0},{8,12},{12,8},{1,5},{5,1},{9,13},{13,9},{2,6},{6,2},{1... | collective-permute-start | bytes 1622024 | tf_op jit(solution)/shard_map/ppermute | solution.py:545
  12.7 0.6 %copy-start.4 = (f32[8,128]{1,0:T(8,128)}, f32[8,128]{1,0:T(8,128)S(1)}, u32[]{:S(2)}) copy-start(f32[8,128]{1,0:T(8,128)S(1)} %collective-permute-done.4.refs_2_.refs_4_) | copy-start | bytes 12292
  12.7 0.6 %copy-start.5 = (f32[8,128]{1,0:T(8,128)}, f32[8,128]{1,0:T(8,128)S(1)}, u32[]{:S(2)}) copy-start(f32[8,128]{1,0:T(8,128)S(1)} %collective-permute-done.3.refs_1_.refs_3_) | copy-start | bytes 12292
  12.7 0.7 %copy-start.3 = (bf16[8,128,128]{2,1,0:T(8,128)(2,1)}, bf16[8,128,128]{2,1,0:T(8,128)(2,1)S(1)}, u32[]{:S(2)}) copy-start(bf16[8,128,128]{2,1,0:T(8,128)(2,1)S(1)} %collective-permute-done.2.other_site.refs_2_) | copy-start | bytes 786436
  13.4 2.3 %copy-start = (bf16[1,8,128,128]{3,2,1,0:T(8,128)(2,1)S(1)}, bf16[1,8,128,128]{3,2,1,0:T(8,128)(2,1)}, u32[]{:S(2)}) copy-start(bf16[1,8,128,128]{3,2,1,0:T(8,128)(2,1)} %param.10) | copy-start | bytes 786436
  13.4 2.3 %copy-start.1 = (f32[1,8,128]{2,1,0:T(8,128)S(1)}, f32[1,8,128]{2,1,0:T(8,128)}, u32[]{:S(2)}) copy-start(f32[1,8,128]{2,1,0:T(8,128)} %param.11) | copy-start | bytes 12292
  13.6 13.4 %collective-permute-start.7 = (bf16[528,128]{1,0:T(8,128)(2,1)S(1)}, bf16[528,128]{1,0:T(8,128)(2,1)S(1)}, u32[]{:S(2)}, u32[]{:S(2)}) collective-permute-start(bf16[528,128]{1,0:T(8,128)(2,1)S(1)} %get-tuple-element.74), channel_id=1, source_target_pairs={{0,4},{4,0},{8,12},{12,8},{1,5},{5,1},{9,13},{13,9},{2,6},{6,2},{1... | collective-permute-start | bytes 405512 | tf_op jit(solution)/shard_map/ppermute | solution.py:545
  14.2 14.3 %collective-permute-start.6 = (bf16[528,128]{1,0:T(8,128)(2,1)S(1)}, bf16[528,128]{1,0:T(8,128)(2,1)S(1)}, u32[]{:S(2)}, u32[]{:S(2)}) collective-permute-start(bf16[528,128]{1,0:T(8,128)(2,1)S(1)} %get-tuple-element.73), channel_id=1, source_target_pairs={{0,4},{4,0},{8,12},{12,8},{1,5},{5,1},{9,13},{13,9},{2,6},{6,2},{1... | collective-permute-start | bytes 405512 | tf_op jit(solution)/shard_map/ppermute | solution.py:545
  29.5 3.1 %collective-permute-start.10 = (f32[2,128]{1,0:T(2,128)S(1)}, f32[2,128]{1,0:T(2,128)S(1)}, u32[]{:S(2)}, u32[]{:S(2)}) collective-permute-start(f32[2,128]{1,0:T(2,128)S(1)} %get-tuple-element.83.refs_0_), channel_id=1, source_target_pairs={{0,3},{1,2},{2,1},{3,0},{4,7},{5,6},{6,5},{7,4},{8,11},{9,10},{10,... | collective-permute-start | bytes 3080 | tf_op jit(solution)/shard_map/ppermute | solution.py:545
  29.6 3.6 %collective-permute-start.9 = (f32[2,128]{1,0:T(2,128)S(1)}, f32[2,128]{1,0:T(2,128)S(1)}, u32[]{:S(2)}, u32[]{:S(2)}) collective-permute-start(f32[2,128]{1,0:T(2,128)S(1)} %get-tuple-element.83.refs_0_), channel_id=1, source_target_pairs={{0,2},{1,3},{2,0},{3,1},{4,6},{5,7},{6,4},{7,5},{8,10},{9,11},{10,... | collective-permute-start | bytes 3080 | tf_op jit(solution)/shard_map/ppermute | solution.py:545
  30.4 2.8 %collective-permute-start.8 = (f32[2,128]{1,0:T(2,128)S(1)}, f32[2,128]{1,0:T(2,128)S(1)}, u32[]{:S(2)}, u32[]{:S(2)}) collective-permute-start(f32[2,128]{1,0:T(2,128)S(1)} %get-tuple-element.83.refs_0_), channel_id=1, source_target_pairs={{0,1},{1,0},{2,3},{3,2},{4,5},{5,4},{6,7},{7,6},{8,9},{9,8},{10,11... | collective-permute-start | bytes 3080 | tf_op jit(solution)/shard_map/ppermute | solution.py:545
  34.5 3.1 %collective-permute-start.13 = (f32[2,128]{1,0:T(2,128)S(1)}, f32[2,128]{1,0:T(2,128)S(1)}, u32[]{:S(2)}, u32[]{:S(2)}) collective-permute-start(f32[2,128]{1,0:T(2,128)S(1)} %get-tuple-element.86.refs_0_), channel_id=1, source_target_pairs={{0,3},{1,2},{2,1},{3,0},{4,7},{5,6},{6,5},{7,4},{8,11},{9,10},{10,... | collective-permute-start | bytes 3080 | tf_op jit(solution)/shard_map/ppermute | solution.py:545
  35.1 3.6 %collective-permute-start.12 = (f32[2,128]{1,0:T(2,128)S(1)}, f32[2,128]{1,0:T(2,128)S(1)}, u32[]{:S(2)}, u32[]{:S(2)}) collective-permute-start(f32[2,128]{1,0:T(2,128)S(1)} %get-tuple-element.86.refs_0_), channel_id=1, source_target_pairs={{0,2},{1,3},{2,0},{3,1},{4,6},{5,7},{6,4},{7,5},{8,10},{9,11},{10,... | collective-permute-start | bytes 3080 | tf_op jit(solution)/shard_map/ppermute | solution.py:545
  35.9 2.8 %collective-permute-start.11 = (f32[2,128]{1,0:T(2,128)S(1)}, f32[2,128]{1,0:T(2,128)S(1)}, u32[]{:S(2)}, u32[]{:S(2)}) collective-permute-start(f32[2,128]{1,0:T(2,128)S(1)} %get-tuple-element.86.refs_0_), channel_id=1, source_target_pairs={{0,1},{1,0},{2,3},{3,2},{4,5},{5,4},{6,7},{7,6},{8,9},{9,8},{10,11... | collective-permute-start | bytes 3080 | tf_op jit(solution)/shard_map/ppermute | solution.py:545
  40.1 3.1 %collective-permute-start.16 = (f32[2,128]{1,0:T(2,128)S(1)}, f32[2,128]{1,0:T(2,128)S(1)}, u32[]{:S(2)}, u32[]{:S(2)}) collective-permute-start(f32[2,128]{1,0:T(2,128)S(1)} %get-tuple-element.89.refs_0_), channel_id=1, source_target_pairs={{0,3},{1,2},{2,1},{3,0},{4,7},{5,6},{6,5},{7,4},{8,11},{9,10},{10,... | collective-permute-start | bytes 3080 | tf_op jit(solution)/shard_map/ppermute | solution.py:545
  40.2 3.6 %collective-permute-start.15 = (f32[2,128]{1,0:T(2,128)S(1)}, f32[2,128]{1,0:T(2,128)S(1)}, u32[]{:S(2)}, u32[]{:S(2)}) collective-permute-start(f32[2,128]{1,0:T(2,128)S(1)} %get-tuple-element.89.refs_0_), channel_id=1, source_target_pairs={{0,2},{1,3},{2,0},{3,1},{4,6},{5,7},{6,4},{7,5},{8,10},{9,11},{10,... | collective-permute-start | bytes 3080 | tf_op jit(solution)/shard_map/ppermute | solution.py:545
  41.0 2.8 %collective-permute-start.14 = (f32[2,128]{1,0:T(2,128)S(1)}, f32[2,128]{1,0:T(2,128)S(1)}, u32[]{:S(2)}, u32[]{:S(2)}) collective-permute-start(f32[2,128]{1,0:T(2,128)S(1)} %get-tuple-element.89.refs_0_), channel_id=1, source_target_pairs={{0,1},{1,0},{2,3},{3,2},{4,5},{5,4},{6,7},{7,6},{8,9},{9,8},{10,11... | collective-permute-start | bytes 3080 | tf_op jit(solution)/shard_map/ppermute | solution.py:545
  45.1 3.1 %collective-permute-start.19 = (f32[2,128]{1,0:T(2,128)S(1)}, f32[2,128]{1,0:T(2,128)S(1)}, u32[]{:S(2)}, u32[]{:S(2)}) collective-permute-start(f32[2,128]{1,0:T(2,128)S(1)} %get-tuple-element.92.refs_0_), channel_id=1, source_target_pairs={{0,3},{1,2},{2,1},{3,0},{4,7},{5,6},{6,5},{7,4},{8,11},{9,10},{10,... | collective-permute-start | bytes 3080 | tf_op jit(solution)/shard_map/ppermute | solution.py:545
  45.7 3.6 %collective-permute-start.18 = (f32[2,128]{1,0:T(2,128)S(1)}, f32[2,128]{1,0:T(2,128)S(1)}, u32[]{:S(2)}, u32[]{:S(2)}) collective-permute-start(f32[2,128]{1,0:T(2,128)S(1)} %get-tuple-element.92.refs_0_), channel_id=1, source_target_pairs={{0,2},{1,3},{2,0},{3,1},{4,6},{5,7},{6,4},{7,5},{8,10},{9,11},{10,... | collective-permute-start | bytes 3080 | tf_op jit(solution)/shard_map/ppermute | solution.py:545
  46.5 2.8 %collective-permute-start.17 = (f32[2,128]{1,0:T(2,128)S(1)}, f32[2,128]{1,0:T(2,128)S(1)}, u32[]{:S(2)}, u32[]{:S(2)}) collective-permute-start(f32[2,128]{1,0:T(2,128)S(1)} %get-tuple-element.92.refs_0_), channel_id=1, source_target_pairs={{0,1},{1,0},{2,3},{3,2},{4,5},{5,4},{6,7},{7,6},{8,9},{9,8},{10,11... | collective-permute-start | bytes 3080 | tf_op jit(solution)/shard_map/ppermute | solution.py:545
  49.6 4.6 %copy-start.2 = (f32[1,128]{1,0:T(1,128)}, f32[1,128]{1,0:T(1,128)S(1)}, u32[]{:S(2)}) copy-start(f32[1,128]{1,0:T(1,128)S(1)} %get-tuple-element.95) | copy-start | bytes 1540
  49.7 3.1 %collective-permute-start.22 = (f32[2,128]{1,0:T(2,128)S(1)}, f32[2,128]{1,0:T(2,128)S(1)}, u32[]{:S(2)}, u32[]{:S(2)}) collective-permute-start(f32[2,128]{1,0:T(2,128)S(1)} %get-tuple-element.94.refs_0_), channel_id=1, source_target_pairs={{0,3},{1,2},{2,1},{3,0},{4,7},{5,6},{6,5},{7,4},{8,11},{9,10},{10,... | collective-permute-start | bytes 3080 | tf_op jit(solution)/shard_map/ppermute | solution.py:545
  49.8 3.6 %collective-permute-start.21 = (f32[2,128]{1,0:T(2,128)S(1)}, f32[2,128]{1,0:T(2,128)S(1)}, u32[]{:S(2)}, u32[]{:S(2)}) collective-permute-start(f32[2,128]{1,0:T(2,128)S(1)} %get-tuple-element.94.refs_0_), channel_id=1, source_target_pairs={{0,2},{1,3},{2,0},{3,1},{4,6},{5,7},{6,4},{7,5},{8,10},{9,11},{10,... | collective-permute-start | bytes 3080 | tf_op jit(solution)/shard_map/ppermute | solution.py:545
  50.6 2.8 %collective-permute-start.20 = (f32[2,128]{1,0:T(2,128)S(1)}, f32[2,128]{1,0:T(2,128)S(1)}, u32[]{:S(2)}, u32[]{:S(2)}) collective-permute-start(f32[2,128]{1,0:T(2,128)S(1)} %get-tuple-element.94.refs_0_), channel_id=1, source_target_pairs={{0,1},{1,0},{2,3},{3,2},{4,5},{5,4},{6,7},{7,6},{8,9},{9,8},{10,11... | collective-permute-start | bytes 3080 | tf_op jit(solution)/shard_map/ppermute | solution.py:545
